TPU v7x, 128 devices: a whole 4x4x4 slice. The times are simulated.
128 devices in a mesh: ctx: 16 (over y, x_hi, core), tp: 8 (over z, x_lo).
Axes of the slice: x: 4 (x_hi: 2, x_lo: 2; x = x_hi * 2 + x_lo), y: 4, z: 4, core: 2. Of those that a mesh axis runs over, the one named last changes fastest.
Arguments:
- text_states: bfloat16 [4096, 8192], P('ctx'), may hold values from -6 to 6
- image_states: bfloat16 [6144, 7680], P('ctx', 'tp'), may hold values from -6 to 6
- counts: int32 [16], replicated, may hold values from 336 to 384, as said below
- norm_gain: float32 [8192], replicated, may hold values from 0.5 to 1.5
- w_query: bfloat16 [8192, 4096], P(None, 'tp'), may hold values from -0.0625 to 0.0625
- q_gain: float32 [128], replicated
- w_key: bfloat16 [7680, 1024], P('tp'), may hold values from -0.09375 to 0.09375
- w_value: bfloat16 [7680, 1024], P('tp'), may hold values from -0.09375 to 0.09375
- k_gain: float32 [128], replicated
- w_out: bfloat16 [4096, 8192], P('tp'), may hold values from -0.125 to 0.125
- attn_gate: float32 [1], replicated, may hold values from 0.3 to 1.2
Outputs:
- layer_out: bfloat16 [4096, 8192], P('ctx', 'tp')
Inputs may be any that keep to these rules, and one draw needn't show every extreme that they name: counts[c] live image slots stand first among the 384 slots of index c of ctx; the rest are padding. counts lie within 48 of 384, and some index has all 384 slots live.
All inputs are finite; a program needn't handle non-finite values.
Results may differ from a plain program's by a relative error of at most 0.0142.
The roundings to bfloat16 on the way count: a program that leaves them out, or rounds other values in their place, can miss the bound.
Values may be sent and summed in bfloat16 or wider, within the bound.
No kernel may reach another device: no remote copies, remote signals or barrier semaphores. Data moves between devices by JAX's collectives and lax.ppermute only.
A program may use at most 128 MiB of HBM per device.

v0:
```python
import jax
import jax.numpy as jnp
from jax import lax
from jax.sharding import PartitionSpec as P

epsilon = 1e-05


def rms_scale(values, scale_gain):
    mean_square = jnp.mean(values * values, axis=-1, keepdims=True)
    return values * lax.rsqrt(mean_square + epsilon) * scale_gain


def live_slots(counts, length, capacity):
    slot_ids = jnp.arange(length, dtype=jnp.int32)
    owner_rank = slot_ids // capacity
    within = slot_ids - owner_rank * capacity
    rank_ids = jnp.arange(counts.shape[0], dtype=jnp.int32)
    slot_limit = jnp.sum(
        jnp.where(owner_rank[:, None] == rank_ids[None, :], counts[None, :], 0), axis=1
    )
    return within < slot_limit


def local(
    text_states,
    image_states,
    counts,
    norm_gain,
    w_query,
    q_gain,
    w_key,
    w_value,
    k_gain,
    w_out,
    attn_gate,
):
    tp_count = lax.axis_size("tp")
    head_dim = q_gain.shape[0]
    capacity = image_states.shape[0]
    local_kv = w_key.shape[1] // head_dim // tp_count
    local_q = w_query.shape[1] // head_dim
    group_size = local_q // local_kv
    tok_rows = text_states.shape[0]
    score_scale = head_dim ** (-0.5)
    part_key = jnp.dot(image_states, w_key, preferred_element_type=jnp.float32)
    part_value = jnp.dot(image_states, w_value, preferred_element_type=jnp.float32)
    key_sum, value_sum = (
        lax.psum_scatter(part_key, "tp", scatter_dimension=1, tiled=True),
        lax.psum_scatter(part_value, "tp", scatter_dimension=1, tiled=True),
    )
    key_rows = rms_scale(key_sum.reshape(capacity, local_kv, head_dim), k_gain).astype(jnp.bfloat16)
    key_rows = key_rows.reshape(capacity, local_kv * head_dim)
    value_rows = value_sum.astype(jnp.bfloat16)
    text_wide = text_states.astype(jnp.float32)
    normed = rms_scale(text_wide, norm_gain).astype(jnp.bfloat16)
    query_rows = jnp.dot(normed, w_query, preferred_element_type=jnp.float32)
    query_rows = rms_scale(
        query_rows.reshape(tok_rows, local_kv, group_size, head_dim), q_gain
    ).astype(jnp.bfloat16)
    all_keys, all_values = (
        lax.all_gather(key_rows, "ctx", axis=0, tiled=True),
        lax.all_gather(value_rows, "ctx", axis=0, tiled=True),
    )
    slot_count = all_keys.shape[0]
    is_live = live_slots(counts, slot_count, capacity)
    score = (
        jnp.einsum(
            "tjgh,sjh->tjgs",
            query_rows,
            all_keys.reshape(slot_count, local_kv, head_dim),
            preferred_element_type=jnp.float32,
        )
        * score_scale
    )
    score = jnp.where(is_live, score, -jnp.inf)
    row_top = jnp.max(score, axis=-1, keepdims=True)
    exp_terms = jnp.exp(score - row_top)
    row_total = jnp.sum(exp_terms, axis=-1)
    weighted = jnp.einsum(
        "tjgs,sjh->tjgh",
        exp_terms.astype(jnp.bfloat16),
        all_values.reshape(slot_count, local_kv, head_dim),
        preferred_element_type=jnp.float32,
    )
    attended = weighted / row_total[..., None]
    attended = attended.astype(jnp.bfloat16).reshape(tok_rows, local_q * head_dim)
    partial_value = jnp.dot(attended, w_out, preferred_element_type=jnp.float32)
    projected = lax.psum_scatter(
        partial_value.astype(jnp.bfloat16), "tp", scatter_dimension=1, tiled=True
    ).astype(jnp.float32)
    own_width = projected.shape[1]
    own_slice = lax.dynamic_slice_in_dim(text_wide, lax.axis_index("tp") * own_width, own_width, 1)
    return (own_slice + jnp.tanh(attn_gate[0]) * projected).astype(jnp.bfloat16)


def solution(mesh):
    in_specs = (
        P("ctx", None),
        P("ctx", "tp"),
        P(),
        P(),
        P(None, "tp"),
        P(),
        P("tp", None),
        P("tp", None),
        P(),
        P("tp", None),
        P(),
    )
    out_specs = P("ctx", "tp")
    return jax.shard_map(local, mesh=mesh, in_specs=in_specs, out_specs=out_specs, check_vma=False)
```

profile of v0, /device:TPU:0, one launch (start us, length us, event | category | flops | bytes accessed | tf_op | source)
XLA Modules:
  0.0 317.7 jit_solution(6670772708430211161)
XLA Ops:
  6.5 1.5 copy-done
  8.1 3.3 %fusion.42 = f32[384,1024]{1,0:T(8,128)} fusion(bf16[384,960]{0,1:T(8,128)(2,1)} %param.12, bf16[960,1024]{1,0:T(8,128)(2,1)S(1)} %copy-done), kind=kOutput, calls=%fused_computation.50 | convolution fusion | flops 754974720 | bytes 4276224 | tf_op jit(solution)/shard_map/dot_general | solution.py:46
  11.4 3.9 %fusion.41 = f32[384,1024]{1,0:T(8,128)} fusion(bf16[384,960]{0,1:T(8,128)(2,1)} %param.12, bf16[960,1024]{1,0:T(8,128)(2,1)} %param.18), kind=kOutput, calls=%fused_computation.49 | convolution fusion | flops 754974720 | bytes 4276224 | tf_op jit(solution)/shard_map/dot_general | solution.py:47
  15.4 43.1 %reduce-scatter.6.cloned.1.call-done = f32[384,128]{1,0:T(8,128)} async-done(((f32[384,1024]{1,0:T(8,128)}), f32[384,128]{1,0:T(8,128)}) %reduce-scatter.6.cloned.1.call-update) | async-done | bytes 196624 | tf_op jit(solution)/shard_map/reduce_scatter | solution.py:49
  58.6 1.1 multiply_reduce_fusion.1
  59.7 1.7 multiply_convert_fusion.2
  61.4 3.1 multiply_reduce_fusion
  64.6 7.2 %fusion.40 = (f32[256,512]{1,0:T(8,128)S(1)}, f32[256,512]{1,0:T(8,128)S(1)}) fusion(bf16[8192,512]{1,0:T(8,128)(2,1)} %param.15, f32[8192]{0:T(1024)S(1)} %copy-done.6, f32[256]{0:T(256)S(1)} %add_rsqrt_fusion.2, bf16[256,8192]{1,0:T(8,128)(2,1)} %param.11), kind=kOutput, calls=%fused_computation.48 | convolution fusion | flops 2156003328 | bytes 13665280 | tf_op jit(solution)/shard_map/dot_general | solution.py:57
  71.8 0.2 mul.122
  72.0 0.3 reduce_sum.48
  72.6 31.8 %reduce-scatter.4.cloned.1.call-done = f32[384,128]{1,0:T(8,128)} async-done(((f32[384,1024]{1,0:T(8,128)}), f32[384,128]{1,0:T(8,128)}) %reduce-scatter.4.cloned.1.call-update) | async-done | bytes 196624 | tf_op jit(solution)/shard_map/reduce_scatter | solution.py:50
  104.4 1.6 convert_element_type.41
  106.0 0.2 reduce-scatter.8.cloned.1.call-start
  106.2 45.7 %all-gather.5.cloned.1.call-done = bf16[6144,128]{1,0:T(8,128)(2,1)} async-done(((bf16[384,128]{1,0:T(8,128)(2,1)}), bf16[6144,128]{1,0:T(8,128)(2,1)}) %all-gather.5.cloned.1.call-update) | async-done | bytes 1572880 | tf_op jit(solution)/shard_map/all_gather | solution.py:62
  151.9 0.3 mul.123
  152.2 4.8 %bitcast_reduce_fusion = (f32[256,4]{0,1:T(4,128)S(1)}, f32[6144,256,4]{1,0,2:T(8,128)S(1)}) fusion(pred[6144]{0:T(1024)(128)(4,1)S(1)} %fusion.36, bf16[6144,128]{1,0:T(8,128)(2,1)} %all-gather.5.cloned.1.call-done, f32[256,512]{1,0:T(8,128)S(1)} %get-tuple-element.6, f32[32,8,4,128]{3,2,1,0:T(4,128)S(1)} %bitcast.99, f32[512]{0:T(512)S(1)} %broadcast_bitcast_fusion), kind=kOutput, calls=%fused_computation.1 | convolution fusion | flops 1629879296 | bytes 27799552 | tf_op jit(solution)/shard_map/tjgh,sjh->tjgs/dot_general | solution.py:68
  157.0 8.4 %copy-done.2 = f32[6144,256,4]{1,0,2:T(8,128)} copy-done((f32[6144,256,4]{1,0,2:T(8,128)}, f32[6144,256,4]{1,0,2:T(8,128)S(1)}, u32[]{:S(2)}) %copy-start.2) | copy-done | bytes 25165848
  165.4 5.5 %fusion.1 = f32[256,4]{0,1:T(4,128)S(1)} fusion(f32[6144,256,4]{1,0,2:T(8,128)S(1)} %get-tuple-element.8, f32[256,4]{0,1:T(4,128)S(1)} %get-tuple-element.7, pred[6144]{0:T(1024)(128)(4,1)S(1)} %fusion.36), kind=kLoop, calls=%fused_computation.4 | loop fusion | flops 25164800 | bytes 25180160 | tf_op jit(solution)/shard_map/reduce_sum | solution.py:79
  170.9 28.2 %all-gather.3.cloned.1.call-done = bf16[6144,128]{1,0:T(8,128)(2,1)} async-done(((bf16[384,128]{1,0:T(8,128)(2,1)}), bf16[6144,128]{1,0:T(8,128)(2,1)}) %all-gather.3.cloned.1.call-update) | async-done | bytes 1572880 | tf_op jit(solution)/shard_map/all_gather | solution.py:63
  199.2 11.5 %fusion.24 = bf16[1,128,256,4]{2,1,3,0:T(8,128)(2,1)S(1)} fusion(f32[6144,256,4]{1,0,2:T(8,128)} %copy-done.2, f32[256,4]{0,1:T(4,128)S(1)} %get-tuple-element.7, pred[6144]{0:T(1024)(128)(4,1)S(1)} %fusion.36, bf16[6144,128]{1,0:T(8,128)(2,1)} %all-gather.3.cloned.1.call-done, f32[256,4]{0,1:T(4,128)S(1)} %fusion.1), kind=kOutput, calls=%fused_computation.22 | convolution fusion | flops 1636040704 | bytes 27015168 | tf_op jit(solution)/shard_map/tjgs,sjh->tjgh/dot_general | solution.py:80
  210.7 7.7 %convolution_convert_fusion = bf16[256,8192]{1,0:T(8,128)(2,1)} fusion(bf16[256,512]{0,1:T(8,128)(2,1)S(1)} %bitcast.100, bf16[512,8192]{1,0:T(8,128)(2,1)} %param.20), kind=kOutput, calls=%fused_computation.9 | convolution fusion | flops 2149580800 | bytes 12845056 | tf_op jit(solution)/shard_map/dot_general | solution.py:88
  218.4 6.5 %convert_element_type.40 = f32[256,8192]{1,0:T(8,128)} convert(bf16[256,8192]{1,0:T(8,128)(2,1)} %param.11) | non-fusion elementwise | flops 2097152 | bytes 12582912 | tf_op jit(solution)/shard_map/convert_element_type | solution.py:55
  225.7 83.2 %reduce-scatter.8.cloned.1.call-done = bf16[256,1024]{1,0:T(8,128)(2,1)} async-done(((bf16[256,8192]{1,0:T(8,128)(2,1)}), bf16[256,1024]{1,0:T(8,128)(2,1)}) %reduce-scatter.8.cloned.1.call-update) | async-done | bytes 524304 | tf_op jit(solution)/shard_map/reduce_scatter | solution.py:89
  308.8 2.3 add_convert_fusion
  (28 shorter events, 0.5 us)
Async XLA Ops:
  6.5 1.5 copy-start
  6.5 53.1 %copy-start.3 = (f32[128]{0:T(128)S(1)}, f32[128]{0:T(128)}, u32[]{:S(2)}) copy-start(f32[128]{0:T(128)} %param.19) | copy-start | bytes 1540
  6.5 58.0 %copy-start.6 = (f32[8192]{0:T(1024)S(1)}, f32[8192]{0:T(1024)}, u32[]{:S(2)}) copy-start(f32[8192]{0:T(1024)} %param.14) | copy-start | bytes 98308
  6.5 52.0 %reduce-scatter.6.cloned.1.call-start = ((), (), s32[]{:S(2)}) async-start(), calls=%async_computation.5 | async-start | bytes 1769472 | tf_op jit(solution)/shard_map/reduce_scatter | solution.py:49
  11.4 93.0 %reduce-scatter.4.cloned.1.call-start = ((), (), s32[]{:S(2)}) async-start(), calls=%async_computation.3 | async-start | bytes 1769472 | tf_op jit(solution)/shard_map/reduce_scatter | solution.py:50
  15.4 136.5 %all-gather.5.cloned.1.call-start = ((), (), s32[]{:S(2)}) async-start(), calls=%async_computation.6 | async-start | bytes 1671168 | tf_op jit(solution)/shard_map/all_gather | solution.py:62
  61.4 137.8 %all-gather.3.cloned.1.call-start = ((), (), s32[]{:S(2)}) async-start(), calls=%async_computation.4 | async-start | bytes 1671168 | tf_op jit(solution)/shard_map/all_gather | solution.py:63
  64.5 7.8 %copy-start.4 = (s32[16]{0:T(128)S(1)}, s32[16]{0:T(128)}, u32[]{:S(2)}) copy-start(s32[16]{0:T(128)} %param.13) | copy-start | bytes 196
  64.6 7.9 %copy-start.5 = (f32[128]{0:T(128)S(1)}, f32[128]{0:T(128)}, u32[]{:S(2)}) copy-start(f32[128]{0:T(128)} %param.16) | copy-start | bytes 1540
  106.0 202.9 %reduce-scatter.8.cloned.1.call-start = ((), (), s32[]{:S(2)}) async-start(), calls=%async_computation.7 | async-start | bytes 4718592 | tf_op jit(solution)/shard_map/reduce_scatter | solution.py:89
  157.0 8.4 %copy-start.2 = (f32[6144,256,4]{1,0,2:T(8,128)}, f32[6144,256,4]{1,0,2:T(8,128)S(1)}, u32[]{:S(2)}) copy-start(f32[6144,256,4]{1,0,2:T(8,128)S(1)} %get-tuple-element.8) | copy-start | bytes 75497472
  218.4 92.7 %copy-start.1 = (bf16[960,1024]{1,0:T(8,128)(2,1)S(1)}, bf16[960,1024]{1,0:T(8,128)(2,1)}, u32[]{:S(2)}) copy-start(bf16[960,1024]{1,0:T(8,128)(2,1)} %param.17) | copy-start | bytes 5898244
Sparse Core Ops, SparseCore 0:
  11.5 47.0 reduce-scatter.5
  61.0 43.3 reduce-scatter.3
  106.8 44.9 all-gather.4
  154.2 44.9 all-gather.2
  218.5 90.2 reduce-scatter.7
where the time goes:
time: 319 us; the launch traced here: 318 us
  waiting for transfers between devices  232 us (73%)
  matrix products  38.4 us (12%)
  other arithmetic  22.3 us (7%)
  between operations  14 us (4%)
  local copies, waits for them, and re-layouts  10.5 us (3%)
    reduce_scatter x1, waiting for transfers between devices, local(): lax.psum_scatter(partial_value.astype(jnp.bfloat16), 'tp', scatter_dimens...  83.2 us
    all_gather x1, waiting for transfers between devices, local(): lax.all_gather(key_rows, 'ctx', axis=0, tiled=True)  45.7 us
    reduce_scatter x1, waiting for transfers between devices, local(): lax.psum_scatter(part_key, 'tp', scatter_dimension=1, tiled=True)  43.1 us
    reduce_scatter x1, waiting for transfers between devices, local(): lax.psum_scatter(part_value, 'tp', scatter_dimension=1, tiled=True)  31.8 us
    all_gather x1, waiting for transfers between devices, local(): lax.all_gather(value_rows, 'ctx', axis=0, tiled=True)  28.2 us
    dot_general x1, matrix products, local(): jnp.einsum('tjgs,sjh->tjgh', exp_terms.astype(jnp.bfloat16), all_values.r...  11.5 us
    unnamed x14, local copies, waits for them, and re-layouts  9.97 us
    dot_general x1, matrix products, local(): partial_value = jnp.dot(attended, w_out, preferred_element_type=jnp.float32)  7.73 us
  transfers between devices with their start and end apart: 5, of which 5 were waited for; matrix products, arithmetic and copies ran while one was open for 11% of the time, Pallas kernels for 0%

commit v1 on v0

v1 whole, which is shorter than its diff:
```python
import functools
import math

import jax
import jax.numpy as jnp
from jax import lax
from jax.experimental import pallas as pl
from jax.experimental.pallas import tpu as pltpu
from jax.sharding import PartitionSpec as P

epsilon = 1e-05
HEAD = 128
TP_SHIFTS = [(2, 1), (2, 0), (1, 1), (3, 1), (1, 0), (3, 0), (0, 1)]
RING = [2, 1, 3]
SMEM = pl.BlockSpec(memory_space=pltpu.SMEM)
VMEM = pl.BlockSpec(memory_space=pltpu.VMEM)
HBM = pl.BlockSpec(memory_space=pltpu.HBM)
HINT = pl.CostEstimate(flops=1 << 20, bytes_accessed=1 << 10, transcendentals=0)


def tp_dest(index, shift):
    return (((index >> 1) + shift[0]) & 3) * 2 + ((index + shift[1]) & 1)


def ctx_dest(index, shift):
    y, xh, core = index >> 2, index >> 1, index
    return ((y + shift[0]) & 3) * 4 + ((xh + shift[1]) & 1) * 2 + ((core + shift[2]) & 1)


def tp_send(block, shift):
    return lax.ppermute(block, "tp", [(i, tp_dest(i, shift)) for i in range(8)])


def ctx_send(block, shift):
    return lax.ppermute(block, "ctx", [(i, ctx_dest(i, shift)) for i in range(16)])


def params(mib=48):
    return pltpu.CompilerParams(vmem_limit_bytes=mib * 1024 * 1024)


def rms_scale(values, scale_gain):
    mean_square = jnp.mean(values * values, axis=-1, keepdims=True)
    return values * lax.rsqrt(mean_square + epsilon) * scale_gain


def kv_kernel(image_ref, key_ref, value_ref, out_ref):
    image = image_ref[...].T
    for head in range(out_ref.shape[0]):
        lanes = slice(head * HEAD, (head + 1) * HEAD)
        weight = jnp.concatenate([key_ref[:, lanes], value_ref[:, lanes]], axis=1)
        out_ref[head] = jnp.dot(image, weight, preferred_element_type=jnp.float32).astype(jnp.bfloat16)


def project_kv(image, w_key, w_value):
    return pl.pallas_call(
        kv_kernel,
        out_shape=jax.ShapeDtypeStruct((w_key.shape[1] // HEAD, image.shape[1], 2 * HEAD), jnp.bfloat16),
        in_specs=[VMEM] * 3,
        out_specs=VMEM,
        compiler_params=params(),
        cost_estimate=HINT,
        name="project_kv",
    )(image, w_key, w_value)


def query_kernel(text_ref, gain_ref, weight_ref, head_gain_ref, out_ref, scale_ref, total_ref):
    step = pl.program_id(0)
    depth = weight_ref.shape[0]
    tiles = text_ref.shape[1] // depth

    @pl.when(step == 0)
    def _():
        square = None
        for at in range(0, text_ref.shape[1], HEAD):
            wide = text_ref[:, at : at + HEAD].astype(jnp.float32)
            square = wide * wide if square is None else square + wide * wide
        mean_square = jnp.sum(square, axis=1, keepdims=True) / text_ref.shape[1]
        scale_ref[...] = jnp.broadcast_to(lax.rsqrt(mean_square + epsilon), scale_ref.shape)

    columns = pl.ds(pl.multiple_of(step * depth, depth), depth)
    wide = text_ref[:, columns].astype(jnp.float32)
    normed = (wide * scale_ref[:, :1] * gain_ref[:, columns]).astype(jnp.bfloat16)
    product = jnp.dot(normed, weight_ref[...], preferred_element_type=jnp.float32)
    total_ref[...] = jnp.where(step == 0, product, total_ref[...] + product)

    @pl.when(step == tiles - 1)
    def _():
        for at in range(0, out_ref.shape[1], HEAD):
            head = total_ref[:, at : at + HEAD]
            out_ref[:, at : at + HEAD] = rms_scale(head, head_gain_ref[...]).astype(jnp.bfloat16)


def project_query(text, norm_gain, w_query, q_gain):
    rows, depth = text.shape
    width, tile = w_query.shape[1], depth // 8
    return pl.pallas_call(
        query_kernel,
        out_shape=jax.ShapeDtypeStruct((rows, width), jnp.bfloat16),
        grid=(depth // tile,),
        in_specs=[
            pl.BlockSpec((rows, depth), lambda step: (0, 0)),
            pl.BlockSpec((1, depth), lambda step: (0, 0)),
            pl.BlockSpec((tile, width), lambda step: (step, 0)),
            pl.BlockSpec((1, HEAD), lambda step: (0, 0)),
        ],
        out_specs=pl.BlockSpec((rows, width), lambda step: (0, 0)),
        scratch_shapes=[pltpu.VMEM((rows, HEAD), jnp.float32), pltpu.VMEM((rows, width), jnp.float32)],
        compiler_params=params(56),
        cost_estimate=HINT,
        name="project_query",
    )(text, norm_gain.reshape(1, depth), w_query, q_gain.reshape(1, HEAD))


def combine_kernel(gain_ref, parts_ref, out_ref):
    total = parts_ref[0].astype(jnp.float32)
    for at in range(1, parts_ref.shape[0]):
        total = total + parts_ref[at].astype(jnp.float32)
    out_ref[:, :HEAD] = rms_scale(total[:, :HEAD], gain_ref[...]).astype(jnp.bfloat16)
    out_ref[:, HEAD:] = total[:, HEAD:].astype(jnp.bfloat16)


def combine_kv(gain, parts):
    return pl.pallas_call(
        combine_kernel,
        out_shape=jax.ShapeDtypeStruct(parts.shape[1:], jnp.bfloat16),
        in_specs=[VMEM] * 2,
        out_specs=VMEM,
        compiler_params=params(),
        cost_estimate=HINT,
        name="combine_kv",
    )(gain.reshape(1, HEAD), parts)


def attend_kernel(shifts, first, last, me_ref, counts_ref, query_ref, *refs):
    stacks, refs = refs[: len(shifts)], refs[len(shifts) :]
    if not first:
        held_in, refs = refs[:3], refs[3:]
    heads = query_ref.shape[1] // HEAD
    capacity = stacks[0].shape[0] // 2
    factor = HEAD ** (-0.5) * math.log2(math.e)
    slot = lax.broadcasted_iota(jnp.int32, (1, HEAD), 1) + (capacity - HEAD)
    for head in range(heads):
        lanes = slice(head * HEAD, (head + 1) * HEAD)
        query = query_ref[:, lanes]
        if not first:
            acc = held_in[0][:, lanes]
            top = held_in[1][:, head : head + 1]
            total = held_in[2][:, head : head + 1]
        for at, ((ring, core), stack) in enumerate(zip(shifts, stacks)):
            score = lax.dot_general(
                query, stack[:, :HEAD], (((1,), (1,)), ((), ())), preferred_element_type=jnp.float32
            )
            pieces = []
            for half in range(2):
                live = slot < counts_ref[ctx_dest(me_ref[0], (-ring, half, core))]
                start, stop = half * capacity, (half + 1) * capacity
                pieces.append(score[:, start : stop - HEAD])
                pieces.append(jnp.where(live, score[:, stop - HEAD : stop], -jnp.inf))
            score = jnp.concatenate(pieces, axis=1)
            block_top = jnp.max(score, axis=1, keepdims=True) * factor
            fresh = first and at == 0
            new_top = block_top if fresh else jnp.maximum(top, block_top)
            weights = jnp.exp2(score * factor - new_top)
            block_total = jnp.sum(weights, axis=1, keepdims=True)
            block_acc = jnp.dot(weights.astype(jnp.bfloat16), stack[:, HEAD:], preferred_element_type=jnp.float32)
            if fresh:
                total, acc = block_total, block_acc
            else:
                decay = jnp.exp2(top - new_top)
                total, acc = total * decay + block_total, acc * decay + block_acc
            top = new_top
        if last:
            refs[0][:, lanes] = (acc / total).astype(jnp.bfloat16)
        else:
            refs[0][:, lanes] = acc
            refs[1][:, head : head + 1] = top
            refs[2][:, head : head + 1] = total


def attend(me, counts, query, blocks, shifts, held, last):
    rows, width = query.shape
    if last:
        out_shape = [jax.ShapeDtypeStruct((rows, width), jnp.bfloat16)]
    else:
        out_shape = [jax.ShapeDtypeStruct((rows, width), jnp.float32)]
        out_shape += [jax.ShapeDtypeStruct((rows, HEAD), jnp.float32)] * 2
    held = list(held or [])
    return pl.pallas_call(
        functools.partial(attend_kernel, shifts, not held, last),
        out_shape=out_shape,
        in_specs=[SMEM, SMEM] + [VMEM] * (1 + len(blocks) + len(held)),
        out_specs=[VMEM] * len(out_shape),
        compiler_params=params(),
        cost_estimate=HINT,
        name="attend",
    )(me, counts, query, *blocks, *held)


def cut_weights(ctx_me, tp_me, w_out):
    rows, tile = w_out.shape[0] // 4, w_out.shape[1] // 16
    y, core, xl = ctx_me >> 2, ctx_me & 1, (tp_me + 1) & 1
    slab = lax.dynamic_slice_in_dim(w_out, y * rows, rows, 0, allow_negative_indices=False)
    first = xl * 2 + core
    return jnp.concatenate(
        [
            lax.dynamic_slice_in_dim(slab, (z * 4 + first) * tile, tile, 1, allow_negative_indices=False)
            for z in range(4)
        ],
        axis=1,
    )


def own_kernel(me_ref, gate_ref, attended_ref, weight_ref, text_ref, *refs):
    outs, (weights, text, sems) = refs[:4], refs[4:]
    width = text.shape[1]
    copies = []
    for at, ring in enumerate(RING + [0]):
        column = pl.multiple_of(tp_dest(me_ref[1], (ring, 0)) * width, width)
        copies.append(pltpu.make_async_copy(weight_ref.at[:, pl.ds(column, width)], weights.at[at], sems.at[at]))
    column = pl.multiple_of(me_ref[1] * width, width)
    copies.append(pltpu.make_async_copy(text_ref.at[:, pl.ds(column, width)], text, sems.at[4]))
    for copy in copies:
        copy.start()
    for at, out in enumerate(outs):
        copies[at].wait()
        total = jnp.dot(attended_ref[...], weights[at], preferred_element_type=jnp.float32)
        if at == 3:
            copies[4].wait()
            total = text[...].astype(jnp.float32) + gate_ref[...] * total
        out[...] = total


def project_own(me, gate, attended, w_out, text):
    rows, width = attended.shape[0], w_out.shape[1] // 8
    return pl.pallas_call(
        own_kernel,
        out_shape=[jax.ShapeDtypeStruct((rows, width), jnp.float32)] * 4,
        in_specs=[SMEM, VMEM, VMEM, HBM, HBM],
        out_specs=[VMEM] * 4,
        scratch_shapes=[
            pltpu.VMEM((4, w_out.shape[0], width), jnp.bfloat16),
            pltpu.VMEM((rows, width), jnp.bfloat16),
            pltpu.SemaphoreType.DMA((5,)),
        ],
        compiler_params=params(32),
        cost_estimate=HINT,
        name="project_own",
    )(me, gate, attended, w_out, text)


def out_kernel(ring, me_ref, gate_ref, swapped_ref, own_ref, *refs):
    mine, other, out = refs[:4], refs[4:8], refs[8]
    y, core, z = me_ref[0] >> 2, me_ref[0] & 1, me_ref[1] >> 1
    rows = mine[0].shape[0]
    tile = mine[0].shape[1] // 4
    swapped = jnp.concatenate(
        [swapped_ref[:, pl.ds(pl.multiple_of(((y - back) & 3) * rows, rows), rows)] for back in [0] + RING], axis=1
    )
    source = pl.ds(pl.multiple_of(((z + ring) & 3) * tile, tile), tile)
    for half, pieces in ((core, mine), (1 - core, other)):
        target = pl.ds(pl.multiple_of(half * tile, tile), tile)
        weight = jnp.concatenate([piece[:, source] for piece in pieces], axis=0)
        product = jnp.dot(swapped, weight, preferred_element_type=jnp.float32)
        if ring == 0:
            product = gate_ref[...] * product
        out[:, target] = (own_ref[:, target] + product).astype(out.dtype)


def project_out(ring, me, gate, swapped, own, mine, other):
    return pl.pallas_call(
        functools.partial(out_kernel, ring),
        out_shape=jax.ShapeDtypeStruct(own.shape, jnp.bfloat16 if ring else jnp.float32),
        in_specs=[SMEM] + [VMEM] * (3 + len(mine) + len(other)),
        out_specs=VMEM,
        compiler_params=params(32),
        cost_estimate=HINT,
        name="project_out",
    )(me, gate, swapped, own, *mine, *other)


def add_kernel(base_ref, gate_ref, *refs):
    total = refs[0][...].astype(jnp.float32)
    for ref in refs[1:-1]:
        total = total + ref[...].astype(jnp.float32)
    refs[-1][...] = (base_ref[...] + gate_ref[...] * total).astype(jnp.bfloat16)


def local(
    text_states,
    image_states,
    counts,
    norm_gain,
    w_query,
    q_gain,
    w_key,
    w_value,
    k_gain,
    w_out,
    attn_gate,
):
    tp_me = lax.axis_index("tp")
    ctx_me = lax.axis_index("ctx")
    ctx_row = ctx_me.astype(jnp.int32).reshape(1)
    me = jnp.stack([ctx_me, tp_me]).astype(jnp.int32)

    cut = cut_weights(ctx_me, tp_me, w_out)
    image_states, text_first, cut = lax.optimization_barrier((image_states, text_states, cut))
    piece = tp_send(cut, (0, 1))
    sent = project_kv(image_states.T, w_key, w_value)
    query = project_query(text_first, norm_gain, w_query, q_gain)
    sent, piece, query = lax.optimization_barrier((sent, piece, query))
    mine = [piece] + [ctx_send(piece, (ring, 0, 0)) for ring in RING]
    arrived = lax.all_to_all(sent, "tp", 0, 0, tiled=True)
    own_kv = combine_kv(k_gain, arrived)

    across = ctx_send(own_kv, (0, 1, 0))
    stack = jnp.concatenate([own_kv, across], axis=0)
    stack, *mine = lax.optimization_barrier((stack, *mine))
    other = [ctx_send(block, (0, 0, 1)) for block in mine]
    far = [ctx_send(stack, (ring, 0, 0)) for ring in RING]
    near = ctx_send(stack, (0, 0, 1))
    held = attend(ctx_row, counts, query, [stack, near], [(0, 0), (0, 1)], None, False)
    *far, held_acc = lax.optimization_barrier((*far, held[0]))
    held = [held_acc, *held[1:]]
    near = [ctx_send(block, (0, 0, 1)) for block in far]
    held = attend(ctx_row, counts, query, far, [(ring, 0) for ring in RING], held, False)
    (attended,) = attend(ctx_row, counts, query, near, [(ring, 1) for ring in RING], held, True)

    gate = jnp.tanh(attn_gate).reshape(1, 1)
    swapped = tp_send(attended, (0, 1))
    own = project_own(me, gate, attended, w_out, text_states)
    arrived = []
    for ring, block in zip(RING, own):
        arrived.append(tp_send(project_out(ring, me, gate, swapped, block, mine, other), (ring, 0)))
    base = project_out(0, me, gate, swapped, own[3], mine, other)
    return pl.pallas_call(
        add_kernel,
        out_shape=jax.ShapeDtypeStruct(base.shape, jnp.bfloat16),
        in_specs=[VMEM] * (2 + len(arrived)),
        out_specs=VMEM,
        compiler_params=params(16),
        cost_estimate=HINT,
        name="add_residual",
    )(base, gate, *arrived)


def solution(mesh):
    in_specs = (
        P("ctx", None),
        P("ctx", "tp"),
        P(),
        P(),
        P(None, "tp"),
        P(),
        P("tp", None),
        P("tp", None),
        P(),
        P("tp", None),
        P(),
    )
    out_specs = P("ctx", "tp")
    return jax.shard_map(local, mesh=mesh, in_specs=in_specs, out_specs=out_specs, check_vma=False)
```

time: 319 us -> 137 us (0.43)
  waiting for transfers between devices: 232 us -> 54.1 us
  Pallas kernels: 0 us -> 44.3 us
  matrix products: 38.4 us -> 0 us
  starting transfers between devices: 0.35 us -> 29.5 us
  other arithmetic: 22.3 us -> 0.15 us
  between operations: 14 us -> 0.87 us
    reduce_scatter x3 -> x0, waiting for transfers between devices: 158 us -> none  [the longest x1 83.2 us: local(): lax.psum_scatter(partial_value.astype(jnp.bfloat16), 'tp', scatter_dimens...]
    all_gather x2 -> x0, waiting for transfers between devices: 73.9 us -> none  [the longest x1 45.7 us: local(): lax.all_gather(key_rows, 'ctx', axis=0, tiled=True)]
    pallas_call x0 -> x12, Pallas kernels: none -> 44.3 us  [the longest x3 18.4 us: attend(): pl.pallas_call(functools.partial(attend_kernel, shifts, not held, last),...]
    ppermute x0 -> x20, waiting for transfers between devices: none -> 39.4 us  [the longest x5 22.7 us: tp_send(): return lax.ppermute(block, 'tp', [(i, tp_dest(i, shift)) for i in range(8)])]
    dot_general x6 -> x0, matrix products: 38.4 us -> none  [the longest x1 11.5 us: local(): jnp.einsum('tjgs,sjh->tjgh', exp_terms.astype(jnp.bfloat16), all_values.r...]
    ppermute x0 -> x20, starting transfers between devices: none -> 24 us  [the longest x15 17.4 us: ctx_send(): lax.ppermute(block, 'ctx', [(i, ctx_dest(i, shift)) for i in range(16)])]
    all_to_all x0 -> x1, waiting for transfers between devices: none -> 14.8 us  [local(): arrived = lax.all_to_all(sent, 'tp', 0, 0, tiled=True)]
    convert_element_type x4 -> x0, other arithmetic: 12.1 us -> none  [the longest x1 6.55 us: local(): text_wide = text_states.astype(jnp.float32)]
  transfers between devices with their start and end apart: 5 -> 21, of which waited for: 5 -> 10; matrix products, arithmetic and copies ran while one was open for 11% -> 0% of each run, Pallas kernels for 0% -> 31%
where the time goes in v1:
time: 137 us; the launch traced here: 136 us
  waiting for transfers between devices  54.1 us (39%)
  Pallas kernels  44.3 us (32%)
  starting transfers between devices  29.5 us (22%)
  local copies, waits for them, and re-layouts  7.54 us (6%)
    ppermute x5, waiting for transfers between devices, tp_send(): return lax.ppermute(block, 'tp', [(i, tp_dest(i, shift)) for i in range(8)])  22.7 us
    pallas_call x3, Pallas kernels, attend(): pl.pallas_call(functools.partial(attend_kernel, shifts, not held, last),...  18.4 us
    ppermute x15, starting transfers between devices, ctx_send(): lax.ppermute(block, 'ctx', [(i, ctx_dest(i, shift)) for i in range(16)])  17.4 us
    ppermute x15, waiting for transfers between devices, ctx_send(): lax.ppermute(block, 'ctx', [(i, ctx_dest(i, shift)) for i in range(16)])  16.7 us
    all_to_all x1, waiting for transfers between devices, local(): arrived = lax.all_to_all(sent, 'tp', 0, 0, tiled=True)  14.8 us
    pallas_call x1, Pallas kernels, project_query(): pl.pallas_call(query_kernel, out_shape=jax.ShapeDtypeStruct((rows, width)...  10.8 us
    ppermute x5, starting transfers between devices, tp_send(): return lax.ppermute(block, 'tp', [(i, tp_dest(i, shift)) for i in range(8)])  6.65 us
    unnamed x14, local copies, waits for them, and re-layouts  6.06 us
  transfers between devices with their start and end apart: 21, of which 10 were waited for; matrix products, arithmetic and copies ran while one was open for 0% of the time, Pallas kernels for 31%

profile of v1, /device:TPU:0, one launch (start us, length us, event | category | flops | bytes accessed | tf_op | source)
XLA Modules:
  0.0 136.5 jit_solution(2798220834099044625)
XLA Ops:
  1.5 1.7 %collective-permute-start = (bf16[128,2048]{1,0:T(8,128)(2,1)S(1)}, bf16[128,2048]{1,0:T(8,128)(2,1)S(1)}, u32[]{:S(2)}, u32[]{:S(2)}) collective-permute-start(bf16[128,2048]{1,0:T(8,128)(2,1)S(1)} %pad_maximum_fusion), channel_id=1, source_target_pairs={{0,1},{1,0},{2,3},{3,2},{4,5},{5,4},{6,7},{7,6},{8,9},{9,8},{10,11... | collective-permute-start | bytes 1572872 | tf_op jit(solution)/shard_map/ppermute | solution.py:31
  3.2 1.5 %copy-done.3 = bf16[960,1024]{1,0:T(8,128)(2,1)S(1)} copy-done((bf16[960,1024]{1,0:T(8,128)(2,1)S(1)}, bf16[960,1024]{1,0:T(8,128)(2,1)}, u32[]{:S(2)}) %copy-start.3) | copy-done | bytes 1966104
  5.9 4.5 %project_kv.1 = bf16[8,384,256]{2,1,0:T(8,128)(2,1)} custom-call(bf16[960,384]{1,0:T(8,128)(2,1)S(1)} %bitcast.7, bf16[960,1024]{1,0:T(8,128)(2,1)S(1)} %copy-done.3, bf16[960,1024]{1,0:T(8,128)(2,1)} %value_ref.1), custom_call_target="tpu_custom_call" | custom-call | flops 1048576 | bytes 1024 | tf_op jit(solution)/shard_map/project_kv/pallas_call | solution.py:56
  10.4 10.8 %project_query.1.query_ref = bf16[256,512]{1,0:T(8,128)(2,1)} custom-call(bf16[256,8192]{1,0:T(8,128)(2,1)} %text_ref.2, f32[1,8192]{1,0:T(1,128)} %bitcast.9, bf16[8192,512]{1,0:T(8,128)(2,1)} %weight_ref.2, f32[1,128]{1,0:T(1,128)} %bitcast.10), custom_call_target="tpu_custom_call" | custom-call | flops 1048576 | bytes 1024 | tf_op jit(solution)/shard_map/project_query/pallas_call | solution.py:97
  21.2 5.5 %all-to-all-start = ((bf16[8,384,256]{2,1,0:T(8,128)(2,1)}), bf16[8,384,256]{2,1,0:T(8,128)(2,1)}, u32[]{:S(2)}, u32[]{:S(2)}) async-start(bf16[8,384,256]{2,1,0:T(8,128)(2,1)} %project_kv.1), calls=%async_computation | async-start | bytes 3145728 | tf_op jit(solution)/shard_map/all_to_all | solution.py:314
  26.7 3.2 %collective-permute-start.2 = (bf16[128,2048]{1,0:T(8,128)(2,1)S(1)}, bf16[128,2048]{1,0:T(8,128)(2,1)S(1)}, u32[]{:S(2)}, u32[]{:S(2)}) collective-permute-start(bf16[128,2048]{1,0:T(8,128)(2,1)S(1)} %collective-permute-done.refs_0_), channel_id=1, source_target_pairs={{0,64},{8,72},{16,80},{24,88},{32,96},{40,104},{48,112},{56,120},{... | collective-permute-start | bytes 1572872 | tf_op jit(solution)/shard_map/ppermute | solution.py:35
  30.5 2.6 %collective-permute-start.4 = (bf16[128,2048]{1,0:T(8,128)(2,1)S(1)}, bf16[128,2048]{1,0:T(8,128)(2,1)S(1)}, u32[]{:S(2)}, u32[]{:S(2)}) collective-permute-start(bf16[128,2048]{1,0:T(8,128)(2,1)S(1)} %collective-permute-done.refs_0_), channel_id=1, source_target_pairs={{0,96},{8,104},{16,112},{24,120},{32,0},{40,8},{48,16},{56,24},{64... | collective-permute-start | bytes 1572872 | tf_op jit(solution)/shard_map/ppermute | solution.py:35
  33.1 14.8 %all-to-all-done.parts_ref = bf16[8,384,256]{2,1,0:T(8,128)(2,1)} async-done(((bf16[8,384,256]{2,1,0:T(8,128)(2,1)}), bf16[8,384,256]{2,1,0:T(8,128)(2,1)}, u32[]{:S(2)}, u32[]{:S(2)}) %all-to-all-start) | async-done | bytes 1572896 | tf_op jit(solution)/shard_map/all_to_all | solution.py:314
  47.8 1.8 %combine_kv.1 = bf16[384,256]{1,0:T(8,128)(2,1)S(1)} custom-call(f32[1,128]{1,0:T(1,128)S(1)} %bitcast.8, bf16[8,384,256]{2,1,0:T(8,128)(2,1)} %all-to-all-done.parts_ref), custom_call_target="tpu_custom_call" | custom-call | flops 1048576 | bytes 1024 | tf_op jit(solution)/shard_map/combine_kv/pallas_call | solution.py:124
  49.7 3.1 %collective-permute-start.1 = (bf16[384,256]{1,0:T(8,128)(2,1)S(1)}, bf16[384,256]{1,0:T(8,128)(2,1)S(1)}, u32[]{:S(2)}, u32[]{:S(2)}) collective-permute-start(bf16[384,256]{1,0:T(8,128)(2,1)S(1)} %combine_kv.1), channel_id=1, source_target_pairs={{0,16},{8,24},{16,0},{24,8},{32,48},{40,56},{48,32},{56,40},{64,80... | collective-permute-start | bytes 589832 | tf_op jit(solution)/shard_map/ppermute | solution.py:35
  52.8 4.2 %collective-permute-done.1 = bf16[384,256]{1,0:T(8,128)(2,1)S(1)} collective-permute-done((bf16[384,256]{1,0:T(8,128)(2,1)S(1)}, bf16[384,256]{1,0:T(8,128)(2,1)S(1)}, u32[]{:S(2)}, u32[]{:S(2)}) %collective-permute-start.1) | collective-permute-done | bytes 196640 | tf_op jit(solution)/shard_map/ppermute | solution.py:35
  57.1 3.3 %collective-permute-start.5 = (bf16[768,256]{1,0:T(8,128)(2,1)S(1)}, bf16[768,256]{1,0:T(8,128)(2,1)S(1)}, u32[]{:S(2)}, u32[]{:S(2)}) collective-permute-start(bf16[768,256]{1,0:T(8,128)(2,1)S(1)} %pad_maximum_fusion.1.refs_0_), channel_id=1, source_target_pairs={{0,64},{8,72},{16,80},{24,88},{32,96},{40,104},{48,112},{56,120},{... | collective-permute-start | bytes 1179656 | tf_op jit(solution)/shard_map/ppermute | solution.py:35
  61.0 2.6 %collective-permute-start.7 = (bf16[768,256]{1,0:T(8,128)(2,1)S(1)}, bf16[768,256]{1,0:T(8,128)(2,1)S(1)}, u32[]{:S(2)}, u32[]{:S(2)}) collective-permute-start(bf16[768,256]{1,0:T(8,128)(2,1)S(1)} %pad_maximum_fusion.1.refs_0_), channel_id=1, source_target_pairs={{0,96},{8,104},{16,112},{24,120},{32,0},{40,8},{48,16},{56,24},{64... | collective-permute-start | bytes 1179656 | tf_op jit(solution)/shard_map/ppermute | solution.py:35
  63.6 3.9 %attend.3 = (f32[256,512]{1,0:T(8,128)S(1)}, f32[256,128]{1,0:T(8,128)S(1)}, f32[256,128]{1,0:T(8,128)S(1)}) custom-call(s32[1]{0:T(128)} %bitcast.me_ref, s32[16]{0:T(128)S(1)} %copy-done.5, bf16[256,512]{1,0:T(8,128)(2,1)S(1)} %copy-done.2, bf16[768,256]{1,0:T(8,128)(2,1)S(1)} %pad_maximum_fusion.1.refs_0_, bf16[768,256]{1,0:T(8,128)(2,1)S(1)} %collective-permute-done.8.refs_1_), custom_call_target="tpu_custom_call" | custom-call | flops 1048576 | bytes 1024 | tf_op jit(solution)/shard_map/attend/pallas_call | solution.py:189
  67.6 3.1 %collective-permute-done.5.refs_0_ = bf16[768,256]{1,0:T(8,128)(2,1)S(1)} collective-permute-done((bf16[768,256]{1,0:T(8,128)(2,1)S(1)}, bf16[768,256]{1,0:T(8,128)(2,1)S(1)}, u32[]{:S(2)}, u32[]{:S(2)}) %collective-permute-start.5) | collective-permute-done | bytes 393248 | tf_op jit(solution)/shard_map/ppermute | solution.py:35
  70.7 7.9 %collective-permute-done.6.refs_1_ = bf16[768,256]{1,0:T(8,128)(2,1)S(1)} collective-permute-done((bf16[768,256]{1,0:T(8,128)(2,1)S(1)}, bf16[768,256]{1,0:T(8,128)(2,1)S(1)}, u32[]{:S(2)}, u32[]{:S(2)}) %collective-permute-start.6) | collective-permute-done | bytes 393248 | tf_op jit(solution)/shard_map/ppermute | solution.py:35
  81.4 7.2 %attend.4 = (f32[256,512]{1,0:T(8,128)S(1)}, f32[256,128]{1,0:T(8,128)S(1)}, f32[256,128]{1,0:T(8,128)S(1)}) custom-call(s32[1]{0:T(128)} %bitcast.me_ref, s32[16]{0:T(128)S(1)} %copy-done.5, bf16[256,512]{1,0:T(8,128)(2,1)S(1)} %copy-done.2, bf16[768,256]{1,0:T(8,128)(2,1)S(1)} %collective-permute-done.5.refs_0_, ...), custom_call_target="tpu_custom_call" | custom-call | flops 1048576 | bytes 1024 | tf_op jit(solution)/shard_map/attend/pallas_call | solution.py:189
  88.5 7.2 %attend.5.attended_ref = bf16[256,512]{1,0:T(8,128)(2,1)S(1)} custom-call(s32[1]{0:T(128)} %bitcast.me_ref, s32[16]{0:T(128)S(1)} %copy-done.5, bf16[256,512]{1,0:T(8,128)(2,1)S(1)} %copy-done.2, bf16[768,256]{1,0:T(8,128)(2,1)S(1)} %collective-permute-done.9.refs_0_, bf16[768,256]{1,0:T(8,128)(2,1)S(1)} %collective-permute-done.10.refs_1_, ...), custom_call_target="tpu_custom_call" | custom-call | flops 1048576 | bytes 1024 | tf_op jit(solution)/shard_map/attend/pallas_call | solution.py:189
  97.7 3.4 %copy-done.1 = bf16[512,8192]{1,0:T(8,128)(2,1)S(1)} copy-done((bf16[512,8192]{1,0:T(8,128)(2,1)S(1)}, bf16[512,8192]{1,0:T(8,128)(2,1)}, u32[]{:S(2)}) %copy-start.1) | copy-done | bytes 8388632
  101.1 3.4 %project_own.1 = (f32[256,1024]{1,0:T(8,128)S(1)}, f32[256,1024]{1,0:T(8,128)S(1)}, f32[256,1024]{1,0:T(8,128)S(1)}, f32[256,1024]{1,0:T(8,128)S(1)}) custom-call(s32[2]{0:T(128)S(1)} %pad_add_fusion.me_ref, f32[1,1]{1,0:T(1,128)} %bitcast.2.gate_ref, bf16[256,512]{1,0:T(8,128)(2,1)S(1)} %attend.5.attended_ref, bf16[512,8192]{1,0:T(8,128)(2,1)S(1)} %copy-done.1, ...), custom_call_target="tpu_custom_call" | custom-call | flops 1048576 | bytes 1024 | tf_op jit(solution)/shard_map/project_own/pallas_call | solution.py:236
  105.7 2.3 %collective-permute-start.19 = (bf16[256,1024]{1,0:T(8,128)(2,1)S(1)}, bf16[256,1024]{1,0:T(8,128)(2,1)S(1)}, u32[]{:S(2)}, u32[]{:S(2)}) collective-permute-start(bf16[256,1024]{1,0:T(8,128)(2,1)S(1)} %project_out.7), channel_id=1, source_target_pairs={{0,6},{1,7},{2,0},{3,1},{4,2},{5,3},{6,4},{7,5},{8,14},{9,15},{10,... | collective-permute-start | bytes 1572872 | tf_op jit(solution)/shard_map/ppermute | solution.py:31
  110.0 1.5 %collective-permute-start.17 = (bf16[256,1024]{1,0:T(8,128)(2,1)S(1)}, bf16[256,1024]{1,0:T(8,128)(2,1)S(1)}, u32[]{:S(2)}, u32[]{:S(2)}) collective-permute-start(bf16[256,1024]{1,0:T(8,128)(2,1)S(1)} %project_out.5), channel_id=1, source_target_pairs={{0,4},{1,5},{2,6},{3,7},{4,0},{5,1},{6,2},{7,3},{8,12},{9,13},{10,... | collective-permute-start | bytes 1572872 | tf_op jit(solution)/shard_map/ppermute | solution.py:31
  112.6 18.1 %collective-permute-done.19.refs_2_ = bf16[256,1024]{1,0:T(8,128)(2,1)S(1)} collective-permute-done((bf16[256,1024]{1,0:T(8,128)(2,1)S(1)}, bf16[256,1024]{1,0:T(8,128)(2,1)S(1)}, u32[]{:S(2)}, u32[]{:S(2)}) %collective-permute-start.19) | collective-permute-done | bytes 524320 | tf_op jit(solution)/shard_map/ppermute | solution.py:31
  130.6 4.5 %collective-permute-done.18.refs_1_ = bf16[256,1024]{1,0:T(8,128)(2,1)S(1)} collective-permute-done((bf16[256,1024]{1,0:T(8,128)(2,1)S(1)}, bf16[256,1024]{1,0:T(8,128)(2,1)S(1)}, u32[]{:S(2)}, u32[]{:S(2)}) %collective-permute-start.18) | collective-permute-done | bytes 524320 | tf_op jit(solution)/shard_map/ppermute | solution.py:31
  (48 shorter events, 13.7 us)
Async XLA Ops:
  1.5 19.6 %collective-permute-start = (bf16[128,2048]{1,0:T(8,128)(2,1)S(1)}, bf16[128,2048]{1,0:T(8,128)(2,1)S(1)}, u32[]{:S(2)}, u32[]{:S(2)}) collective-permute-start(bf16[128,2048]{1,0:T(8,128)(2,1)S(1)} %pad_maximum_fusion), channel_id=1, source_target_pairs={{0,1},{1,0},{2,3},{3,2},{4,5},{5,4},{6,7},{7,6},{8,9},{9,8},{10,11... | collective-permute-start | bytes 1572872 | tf_op jit(solution)/shard_map/ppermute | solution.py:31
  21.2 42.4 %copy-start.2 = (bf16[256,512]{1,0:T(8,128)(2,1)S(1)}, bf16[256,512]{1,0:T(8,128)(2,1)}, u32[]{:S(2)}) copy-start(bf16[256,512]{1,0:T(8,128)(2,1)} %project_query.1.query_ref) | copy-start | bytes 786436
  21.2 42.4 %copy-start.5 = (s32[16]{0:T(128)S(1)}, s32[16]{0:T(128)}, u32[]{:S(2)}) copy-start(s32[16]{0:T(128)} %counts_ref.5) | copy-start | bytes 196
  21.2 26.6 %all-to-all-start = ((bf16[8,384,256]{2,1,0:T(8,128)(2,1)}), bf16[8,384,256]{2,1,0:T(8,128)(2,1)}, u32[]{:S(2)}, u32[]{:S(2)}) async-start(bf16[8,384,256]{2,1,0:T(8,128)(2,1)} %project_kv.1), calls=%async_computation | async-start | bytes 3145728 | tf_op jit(solution)/shard_map/all_to_all | solution.py:314
  26.7 30.3 %collective-permute-start.2 = (bf16[128,2048]{1,0:T(8,128)(2,1)S(1)}, bf16[128,2048]{1,0:T(8,128)(2,1)S(1)}, u32[]{:S(2)}, u32[]{:S(2)}) collective-permute-start(bf16[128,2048]{1,0:T(8,128)(2,1)S(1)} %collective-permute-done.refs_0_), channel_id=1, source_target_pairs={{0,64},{8,72},{16,80},{24,88},{32,96},{40,104},{48,112},{56,120},{... | collective-permute-start | bytes 1572872 | tf_op jit(solution)/shard_map/ppermute | solution.py:35
  29.9 27.1 %collective-permute-start.3 = (bf16[128,2048]{1,0:T(8,128)(2,1)S(1)}, bf16[128,2048]{1,0:T(8,128)(2,1)S(1)}, u32[]{:S(2)}, u32[]{:S(2)}) collective-permute-start(bf16[128,2048]{1,0:T(8,128)(2,1)S(1)} %collective-permute-done.refs_0_), channel_id=1, source_target_pairs={{0,32},{8,40},{16,48},{24,56},{32,64},{40,72},{48,80},{56,88},{64,... | collective-permute-start | bytes 1572872 | tf_op jit(solution)/shard_map/ppermute | solution.py:35
  30.5 26.5 %collective-permute-start.4 = (bf16[128,2048]{1,0:T(8,128)(2,1)S(1)}, bf16[128,2048]{1,0:T(8,128)(2,1)S(1)}, u32[]{:S(2)}, u32[]{:S(2)}) collective-permute-start(bf16[128,2048]{1,0:T(8,128)(2,1)S(1)} %collective-permute-done.refs_0_), channel_id=1, source_target_pairs={{0,96},{8,104},{16,112},{24,120},{32,0},{40,8},{48,16},{56,24},{64... | collective-permute-start | bytes 1572872 | tf_op jit(solution)/shard_map/ppermute | solution.py:35
  47.8 49.8 %copy-start = (bf16[256,8192]{1,0:T(8,128)(2,1)S(1)}, bf16[256,8192]{1,0:T(8,128)(2,1)}, u32[]{:S(2)}) copy-start(bf16[256,8192]{1,0:T(8,128)(2,1)} %text_ref.2) | copy-start | bytes 12582916
  49.7 7.3 %collective-permute-start.1 = (bf16[384,256]{1,0:T(8,128)(2,1)S(1)}, bf16[384,256]{1,0:T(8,128)(2,1)S(1)}, u32[]{:S(2)}, u32[]{:S(2)}) collective-permute-start(bf16[384,256]{1,0:T(8,128)(2,1)S(1)} %combine_kv.1), channel_id=1, source_target_pairs={{0,16},{8,24},{16,0},{24,8},{32,48},{40,56},{48,32},{56,40},{64,80... | collective-permute-start | bytes 589832 | tf_op jit(solution)/shard_map/ppermute | solution.py:35
  57.0 6.6 %collective-permute-start.8 = (bf16[768,256]{1,0:T(8,128)(2,1)S(1)}, bf16[768,256]{1,0:T(8,128)(2,1)S(1)}, u32[]{:S(2)}, u32[]{:S(2)}) collective-permute-start(bf16[768,256]{1,0:T(8,128)(2,1)S(1)} %pad_maximum_fusion.1.refs_0_), channel_id=1, source_target_pairs={{0,8},{8,0},{16,24},{24,16},{32,40},{40,32},{48,56},{56,48},{64,72... | collective-permute-start | bytes 1179656 | tf_op jit(solution)/shard_map/ppermute | solution.py:35
  57.1 13.6 %collective-permute-start.5 = (bf16[768,256]{1,0:T(8,128)(2,1)S(1)}, bf16[768,256]{1,0:T(8,128)(2,1)S(1)}, u32[]{:S(2)}, u32[]{:S(2)}) collective-permute-start(bf16[768,256]{1,0:T(8,128)(2,1)S(1)} %pad_maximum_fusion.1.refs_0_), channel_id=1, source_target_pairs={{0,64},{8,72},{16,80},{24,88},{32,96},{40,104},{48,112},{56,120},{... | collective-permute-start | bytes 1179656 | tf_op jit(solution)/shard_map/ppermute | solution.py:35
  60.4 18.2 %collective-permute-start.6 = (bf16[768,256]{1,0:T(8,128)(2,1)S(1)}, bf16[768,256]{1,0:T(8,128)(2,1)S(1)}, u32[]{:S(2)}, u32[]{:S(2)}) collective-permute-start(bf16[768,256]{1,0:T(8,128)(2,1)S(1)} %pad_maximum_fusion.1.refs_0_), channel_id=1, source_target_pairs={{0,32},{8,40},{16,48},{24,56},{32,64},{40,72},{48,80},{56,88},{64,... | collective-permute-start | bytes 1179656 | tf_op jit(solution)/shard_map/ppermute | solution.py:35
  61.0 17.9 %collective-permute-start.7 = (bf16[768,256]{1,0:T(8,128)(2,1)S(1)}, bf16[768,256]{1,0:T(8,128)(2,1)S(1)}, u32[]{:S(2)}, u32[]{:S(2)}) collective-permute-start(bf16[768,256]{1,0:T(8,128)(2,1)S(1)} %pad_maximum_fusion.1.refs_0_), channel_id=1, source_target_pairs={{0,96},{8,104},{16,112},{24,120},{32,0},{40,8},{48,16},{56,24},{64... | collective-permute-start | bytes 1179656 | tf_op jit(solution)/shard_map/ppermute | solution.py:35
  78.9 1.7 %collective-permute-start.10 = (bf16[768,256]{1,0:T(8,128)(2,1)S(1)}, bf16[768,256]{1,0:T(8,128)(2,1)S(1)}, u32[]{:S(2)}, u32[]{:S(2)}) collective-permute-start(bf16[768,256]{1,0:T(8,128)(2,1)S(1)} %collective-permute-done.6.refs_1_), channel_id=1, source_target_pairs={{0,8},{8,0},{16,24},{24,16},{32,40},{40,32},{48,56},{56,48},{64,72... | collective-permute-start | bytes 1179656 | tf_op jit(solution)/shard_map/ppermute | solution.py:35
  78.9 2.3 %collective-permute-start.11 = (bf16[768,256]{1,0:T(8,128)(2,1)S(1)}, bf16[768,256]{1,0:T(8,128)(2,1)S(1)}, u32[]{:S(2)}, u32[]{:S(2)}) collective-permute-start(bf16[768,256]{1,0:T(8,128)(2,1)S(1)} %collective-permute-done.7.refs_2_), channel_id=1, source_target_pairs={{0,8},{8,0},{16,24},{24,16},{32,40},{40,32},{48,56},{56,48},{64,72... | collective-permute-start | bytes 1179656 | tf_op jit(solution)/shard_map/ppermute | solution.py:35
  79.4 9.1 %collective-permute-start.9 = (bf16[768,256]{1,0:T(8,128)(2,1)S(1)}, bf16[768,256]{1,0:T(8,128)(2,1)S(1)}, u32[]{:S(2)}, u32[]{:S(2)}) collective-permute-start(bf16[768,256]{1,0:T(8,128)(2,1)S(1)} %collective-permute-done.5.refs_0_), channel_id=1, source_target_pairs={{0,8},{8,0},{16,24},{24,16},{32,40},{40,32},{48,56},{56,48},{64,72... | collective-permute-start | bytes 1179656 | tf_op jit(solution)/shard_map/ppermute | solution.py:35
  79.4 25.0 %collective-permute-start.13 = (bf16[128,2048]{1,0:T(8,128)(2,1)S(1)}, bf16[128,2048]{1,0:T(8,128)(2,1)S(1)}, u32[]{:S(2)}, u32[]{:S(2)}) collective-permute-start(bf16[128,2048]{1,0:T(8,128)(2,1)S(1)} %collective-permute-done.refs_0_), channel_id=1, source_target_pairs={{0,8},{8,0},{16,24},{24,16},{32,40},{40,32},{48,56},{56,48},{64,72... | collective-permute-start | bytes 1572872 | tf_op jit(solution)/shard_map/ppermute | solution.py:35
  80.0 24.6 %collective-permute-start.14 = (bf16[128,2048]{1,0:T(8,128)(2,1)S(1)}, bf16[128,2048]{1,0:T(8,128)(2,1)S(1)}, u32[]{:S(2)}, u32[]{:S(2)}) collective-permute-start(bf16[128,2048]{1,0:T(8,128)(2,1)S(1)} %collective-permute-done.2.refs_1_), channel_id=1, source_target_pairs={{0,8},{8,0},{16,24},{24,16},{32,40},{40,32},{48,56},{56,48},{64,72... | collective-permute-start | bytes 1572872 | tf_op jit(solution)/shard_map/ppermute | solution.py:35
  80.7 23.9 %collective-permute-start.15 = (bf16[128,2048]{1,0:T(8,128)(2,1)S(1)}, bf16[128,2048]{1,0:T(8,128)(2,1)S(1)}, u32[]{:S(2)}, u32[]{:S(2)}) collective-permute-start(bf16[128,2048]{1,0:T(8,128)(2,1)S(1)} %collective-permute-done.3.refs_2_), channel_id=1, source_target_pairs={{0,8},{8,0},{16,24},{24,16},{32,40},{40,32},{48,56},{56,48},{64,72... | collective-permute-start | bytes 1572872 | tf_op jit(solution)/shard_map/ppermute | solution.py:35
  81.2 23.3 %collective-permute-start.16 = (bf16[128,2048]{1,0:T(8,128)(2,1)S(1)}, bf16[128,2048]{1,0:T(8,128)(2,1)S(1)}, u32[]{:S(2)}, u32[]{:S(2)}) collective-permute-start(bf16[128,2048]{1,0:T(8,128)(2,1)S(1)} %collective-permute-done.4.refs_3_), channel_id=1, source_target_pairs={{0,8},{8,0},{16,24},{24,16},{32,40},{40,32},{48,56},{56,48},{64,72... | collective-permute-start | bytes 1572872 | tf_op jit(solution)/shard_map/ppermute | solution.py:35
  95.8 8.9 %collective-permute-start.12 = (bf16[256,512]{1,0:T(8,128)(2,1)S(1)}, bf16[256,512]{1,0:T(8,128)(2,1)S(1)}, u32[]{:S(2)}, u32[]{:S(2)}) collective-permute-start(bf16[256,512]{1,0:T(8,128)(2,1)S(1)} %attend.5.attended_ref), channel_id=1, source_target_pairs={{0,1},{1,0},{2,3},{3,2},{4,5},{5,4},{6,7},{7,6},{8,9},{9,8},{10,11... | collective-permute-start | bytes 786440 | tf_op jit(solution)/shard_map/ppermute | solution.py:31
  105.7 25.0 %collective-permute-start.19 = (bf16[256,1024]{1,0:T(8,128)(2,1)S(1)}, bf16[256,1024]{1,0:T(8,128)(2,1)S(1)}, u32[]{:S(2)}, u32[]{:S(2)}) collective-permute-start(bf16[256,1024]{1,0:T(8,128)(2,1)S(1)} %project_out.7), channel_id=1, source_target_pairs={{0,6},{1,7},{2,0},{3,1},{4,2},{5,3},{6,4},{7,5},{8,14},{9,15},{10,... | collective-permute-start | bytes 1572872 | tf_op jit(solution)/shard_map/ppermute | solution.py:31
  108.9 26.2 %collective-permute-start.18 = (bf16[256,1024]{1,0:T(8,128)(2,1)S(1)}, bf16[256,1024]{1,0:T(8,128)(2,1)S(1)}, u32[]{:S(2)}, u32[]{:S(2)}) collective-permute-start(bf16[256,1024]{1,0:T(8,128)(2,1)S(1)} %project_out.6), channel_id=1, source_target_pairs={{0,2},{1,3},{2,4},{3,5},{4,6},{5,7},{6,0},{7,1},{8,10},{9,11},{10,... | collective-permute-start | bytes 1572872 | tf_op jit(solution)/shard_map/ppermute | solution.py:31
  110.0 25.1 %collective-permute-start.17 = (bf16[256,1024]{1,0:T(8,128)(2,1)S(1)}, bf16[256,1024]{1,0:T(8,128)(2,1)S(1)}, u32[]{:S(2)}, u32[]{:S(2)}) collective-permute-start(bf16[256,1024]{1,0:T(8,128)(2,1)S(1)} %project_out.5), channel_id=1, source_target_pairs={{0,4},{1,5},{2,6},{3,7},{4,0},{5,1},{6,2},{7,3},{8,12},{9,13},{10,... | collective-permute-start | bytes 1572872 | tf_op jit(solution)/shard_map/ppermute | solution.py:31
  (4 other events, 43.5 us)

commit v2 on v1

v2 whole, which is shorter than its diff:
```python
import functools
import math

import jax
import jax.numpy as jnp
from jax import lax
from jax.experimental import pallas as pl
from jax.experimental.pallas import tpu as pltpu
from jax.sharding import PartitionSpec as P

epsilon = 1e-05
HEAD = 128
TP_SHIFTS = [(2, 1), (2, 0), (1, 1), (3, 1), (1, 0), (3, 0), (0, 1)]
RING = [2, 1, 3]
HOPS = [1, 2, 3, 0]
AROUND = [(2, 1), (0, 1), (1, 0), (3, 0), (2, 0), (1, 1), (3, 1), (0, 0)]
SMEM = pl.BlockSpec(memory_space=pltpu.SMEM)
VMEM = pl.BlockSpec(memory_space=pltpu.VMEM)
HBM = pl.BlockSpec(memory_space=pltpu.HBM)
HINT = pl.CostEstimate(flops=1 << 20, bytes_accessed=1 << 10, transcendentals=0)


def tp_dest(index, shift):
    return (((index >> 1) + shift[0]) & 3) * 2 + ((index + shift[1]) & 1)


def ctx_dest(index, shift):
    y, xh, core = index >> 2, index >> 1, index
    return ((y + shift[0]) & 3) * 4 + ((xh + shift[1]) & 1) * 2 + ((core + shift[2]) & 1)


def tp_send(block, shift):
    return lax.ppermute(block, "tp", [(i, tp_dest(i, shift)) for i in range(8)])


def hop_send(block, hop):
    return lax.ppermute(block, "tp", [(i, i ^ (2 * hop)) for i in range(8)])


def ctx_send(block, shift):
    return lax.ppermute(block, "ctx", [(i, ctx_dest(i, shift)) for i in range(16)])


def params(mib=48):
    return pltpu.CompilerParams(vmem_limit_bytes=mib * 1024 * 1024)


def rms_scale(values, scale_gain):
    mean_square = jnp.mean(values * values, axis=-1, keepdims=True)
    return values * lax.rsqrt(mean_square + epsilon) * scale_gain


def kv_kernel(image_ref, key_ref, value_ref, out_ref):
    image = image_ref[...].T
    for head in range(out_ref.shape[0]):
        lanes = slice(head * HEAD, (head + 1) * HEAD)
        weight = jnp.concatenate([key_ref[:, lanes], value_ref[:, lanes]], axis=1)
        out_ref[head] = jnp.dot(image, weight, preferred_element_type=jnp.float32).astype(jnp.bfloat16)


def project_kv(image, w_key, w_value):
    return pl.pallas_call(
        kv_kernel,
        out_shape=jax.ShapeDtypeStruct((w_key.shape[1] // HEAD, image.shape[1], 2 * HEAD), jnp.bfloat16),
        in_specs=[VMEM] * 3,
        out_specs=VMEM,
        compiler_params=params(),
        cost_estimate=HINT,
        name="project_kv",
    )(image, w_key, w_value)


def query_kernel(text_ref, gain_ref, weight_ref, head_gain_ref, out_ref, scale_ref, total_ref):
    step = pl.program_id(0)
    depth = weight_ref.shape[0]
    tiles = text_ref.shape[1] // depth

    @pl.when(step == 0)
    def _():
        square = None
        for at in range(0, text_ref.shape[1], HEAD):
            wide = text_ref[:, at : at + HEAD].astype(jnp.float32)
            square = wide * wide if square is None else square + wide * wide
        mean_square = jnp.sum(square, axis=1, keepdims=True) / text_ref.shape[1]
        scale_ref[...] = jnp.broadcast_to(lax.rsqrt(mean_square + epsilon), scale_ref.shape)

    columns = pl.ds(pl.multiple_of(step * depth, depth), depth)
    wide = text_ref[:, columns].astype(jnp.float32)
    normed = (wide * scale_ref[:, :1] * gain_ref[:, columns]).astype(jnp.bfloat16)
    product = jnp.dot(normed, weight_ref[...], preferred_element_type=jnp.float32)
    total_ref[...] = jnp.where(step == 0, product, total_ref[...] + product)

    @pl.when(step == tiles - 1)
    def _():
        rows = total_ref.shape[0]
        for at in range(total_ref.shape[1] // HEAD):
            head = total_ref[:, at * HEAD : (at + 1) * HEAD]
            out_ref[at * rows : (at + 1) * rows] = rms_scale(head, head_gain_ref[...]).astype(jnp.bfloat16)


def project_query(text, norm_gain, w_query, q_gain):
    rows, depth = text.shape
    width, tile = w_query.shape[1], depth // 8
    return pl.pallas_call(
        query_kernel,
        out_shape=jax.ShapeDtypeStruct((rows * width // HEAD, HEAD), jnp.bfloat16),
        grid=(depth // tile,),
        in_specs=[
            pl.BlockSpec((rows, depth), lambda step: (0, 0)),
            pl.BlockSpec((1, depth), lambda step: (0, 0)),
            pl.BlockSpec((tile, width), lambda step: (step, 0)),
            pl.BlockSpec((1, HEAD), lambda step: (0, 0)),
        ],
        out_specs=pl.BlockSpec((rows * width // HEAD, HEAD), lambda step: (0, 0)),
        scratch_shapes=[pltpu.VMEM((rows, HEAD), jnp.float32), pltpu.VMEM((rows, width), jnp.float32)],
        compiler_params=params(32),
        cost_estimate=HINT,
        name="project_query",
    )(text, norm_gain.reshape(1, depth), w_query, q_gain.reshape(1, HEAD))


def combine_kernel(gain_ref, parts_ref, out_ref):
    total = parts_ref[0].astype(jnp.float32)
    for at in range(1, parts_ref.shape[0]):
        total = total + parts_ref[at].astype(jnp.float32)
    keys = rms_scale(total[:, :HEAD], gain_ref[...]).astype(jnp.bfloat16)
    values = total[:, HEAD:].astype(jnp.bfloat16)
    out_ref[:, :HEAD] = keys
    out_ref[:, HEAD:] = values


def combine_kv(gain, parts):
    return pl.pallas_call(
        combine_kernel,
        out_shape=jax.ShapeDtypeStruct(parts.shape[1:], jnp.bfloat16),
        in_specs=[VMEM] * 2,
        out_specs=VMEM,
        compiler_params=params(),
        cost_estimate=HINT,
        name="combine_kv",
    )(gain.reshape(1, HEAD), parts)


def attend_kernel(flip, last, me_ref, counts_ref, query_ref, *refs):
    first = not last
    blocks, refs = refs[: len(AROUND)], refs[len(AROUND) :]
    if not first:
        held_in, refs = refs[:2], refs[2:]
    outs, (score_ref,) = refs[:-1], refs[-1:]
    capacity = blocks[0].shape[0]
    slots = len(blocks) * capacity
    factor = HEAD ** (-0.5) * math.log2(math.e)
    slot = lax.broadcasted_iota(jnp.int32, (1, HEAD), 1) + (capacity - HEAD)
    keys = jnp.concatenate([block[:, :HEAD] for block in blocks], axis=0)
    values = jnp.concatenate([block[:, HEAD:] for block in blocks], axis=0)
    values = jnp.concatenate([values, jnp.ones_like(values)], axis=1)
    score_ref[...] = lax.dot_general(
        query_ref[...], keys, (((1,), (1,)), ((), ())), preferred_element_type=jnp.float32
    )
    live = [slot < counts_ref[ctx_dest(me_ref[0], (-y, -xh, flip))] for y, xh in AROUND]
    rows = 256
    for start in range(0, query_ref.shape[0], rows):
        band = slice(start, start + rows)
        pieces = []
        for at in range(0, slots, HEAD):
            piece = score_ref[band, at : at + HEAD]
            if at % capacity == capacity - HEAD:
                piece = jnp.where(live[at // capacity], piece, -jnp.inf)
            pieces.append(piece)
        top = functools.reduce(jnp.maximum, pieces)
        top = jnp.max(top, axis=1, keepdims=True) * factor
        if not first:
            top = jnp.maximum(held_in[1][band, :1], top)
        weights = [jnp.exp2(piece * factor - top).astype(jnp.bfloat16) for piece in pieces]
        acc = jnp.dot(jnp.concatenate(weights, axis=1), values, preferred_element_type=jnp.float32)
        if not first:
            acc = acc + held_in[0][band] * jnp.exp2(held_in[1][band, :1] - top)
        if last:
            lanes = slice(start // rows * HEAD, (start // rows + 1) * HEAD)
            outs[0][:, lanes] = (acc[:, :HEAD] / acc[:, HEAD:]).astype(jnp.bfloat16)
        else:
            outs[0][band] = acc
            outs[1][band] = jnp.broadcast_to(top, (rows, HEAD))


def attend(me, counts, query, blocks, flip, held=()):
    rows = query.shape[0]
    if held:
        out_shape = [jax.ShapeDtypeStruct((256, rows * HEAD // 256), jnp.bfloat16)]
    else:
        out_shape = [jax.ShapeDtypeStruct((rows, width), jnp.float32) for width in (2 * HEAD, HEAD)]
    return pl.pallas_call(
        functools.partial(attend_kernel, flip, bool(held)),
        out_shape=out_shape,
        in_specs=[SMEM, SMEM] + [VMEM] * (1 + len(blocks) + len(held)),
        out_specs=[VMEM] * len(out_shape),
        scratch_shapes=[pltpu.VMEM((rows, len(blocks) * blocks[0].shape[0]), jnp.float32)],
        compiler_params=params(),
        cost_estimate=HINT,
        name="attend",
    )(me, counts, query, *blocks, *held)


def cut_weights(ctx_me, tp_me, w_out):
    rows, tile = w_out.shape[0] // 4, w_out.shape[1] // 16
    y, core, xl = ctx_me >> 2, ctx_me & 1, (tp_me + 1) & 1
    slab = lax.dynamic_slice_in_dim(w_out, y * rows, rows, 0, allow_negative_indices=False)
    first = xl * 2 + core
    return jnp.concatenate(
        [
            lax.dynamic_slice_in_dim(slab, (z * 4 + first) * tile, tile, 1, allow_negative_indices=False)
            for z in range(4)
        ],
        axis=1,
    )


def own_kernel(me_ref, gate_ref, attended_ref, weight_ref, text_ref, *refs):
    outs, (weights, text, sems) = refs[:4], refs[4:]
    width = text.shape[1]
    copies = []
    for at, hop in enumerate(HOPS):
        column = pl.multiple_of((me_ref[1] ^ (2 * hop)) * width, width)
        copies.append(pltpu.make_async_copy(weight_ref.at[:, pl.ds(column, width)], weights.at[at], sems.at[at]))
    column = pl.multiple_of(me_ref[1] * width, width)
    copies.append(pltpu.make_async_copy(text_ref.at[:, pl.ds(column, width)], text, sems.at[4]))
    for copy in copies:
        copy.start()
    for at, (hop, out) in enumerate(zip(HOPS, outs)):
        copies[at].wait()
        total = jnp.dot(attended_ref[...], weights[at], preferred_element_type=jnp.float32)
        if hop == 0:
            copies[4].wait()
            total = text[...].astype(jnp.float32) + gate_ref[...] * total
        out[...] = total


def project_own(me, gate, attended, w_out, text):
    rows, width = attended.shape[0], w_out.shape[1] // 8
    return pl.pallas_call(
        own_kernel,
        out_shape=[jax.ShapeDtypeStruct((rows, width), jnp.float32)] * 4,
        in_specs=[SMEM, VMEM, VMEM, HBM, HBM],
        out_specs=[VMEM] * 4,
        scratch_shapes=[
            pltpu.VMEM((4, w_out.shape[0], width), jnp.bfloat16),
            pltpu.VMEM((rows, width), jnp.bfloat16),
            pltpu.SemaphoreType.DMA((5,)),
        ],
        compiler_params=params(46),
        cost_estimate=HINT,
        name="project_own",
    )(me, gate, attended, w_out, text)


def out_kernel(jobs, me_ref, gate_ref, swapped_ref, *refs):
    own, mine, other, outs = refs[:4], refs[4:8], refs[8:12], refs[12:]
    y, core, z = me_ref[0] >> 2, me_ref[0] & 1, me_ref[1] >> 1
    rows = mine[0].shape[0]
    tile = mine[0].shape[1] // 4
    swapped = jnp.concatenate(
        [swapped_ref[:, pl.ds(pl.multiple_of(((y - back) & 3) * rows, rows), rows)] for back in [0] + RING], axis=1
    )
    for (hops, start, stop), out in zip(jobs, outs):
        for at, hop in enumerate(hops):
            source = pl.ds(pl.multiple_of((z ^ hop) * tile, tile), tile)
            band = slice(at * (stop - start), (at + 1) * (stop - start))
            for half, pieces in ((core, mine), (1 - core, other)):
                target = pl.ds(pl.multiple_of(half * tile, tile), tile)
                weight = jnp.concatenate([piece[:, source] for piece in pieces], axis=0)
                product = jnp.dot(swapped[start:stop], weight, preferred_element_type=jnp.float32)
                if hop == 0:
                    product = gate_ref[...] * product
                total = own[HOPS.index(hop)][start:stop, target] + product
                out[band, target] = total.astype(out.dtype)


def project_out(jobs, dtype, me, gate, swapped, own, mine, other):
    width = own[0].shape[1]
    return pl.pallas_call(
        functools.partial(out_kernel, jobs),
        out_shape=[jax.ShapeDtypeStruct((len(hops) * (stop - start), width), dtype) for hops, start, stop in jobs],
        in_specs=[SMEM] + [VMEM] * 14,
        out_specs=[VMEM] * len(jobs),
        compiler_params=params(32),
        cost_estimate=HINT,
        name="project_out",
    )(me, gate, swapped, *own, *mine, *other)


def relay_kernel(kept_ref, arrived_ref, out_ref):
    rows = out_ref.shape[0]
    out_ref[...] = (kept_ref[...] + arrived_ref[rows:].astype(jnp.float32)).astype(out_ref.dtype)


def relay(kept, arrived):
    return pl.pallas_call(
        relay_kernel,
        out_shape=jax.ShapeDtypeStruct(kept.shape, jnp.bfloat16),
        in_specs=[VMEM] * 2,
        out_specs=VMEM,
        compiler_params=params(16),
        cost_estimate=HINT,
        name="relay",
    )(kept, arrived)


def add_kernel(base_ref, gate_ref, *refs):
    arrived, out_ref = refs[:-1], refs[-1]
    rows = out_ref.shape[0] // 2
    for at in range(2):
        band = slice(at * rows, (at + 1) * rows)
        total = arrived[at][:rows].astype(jnp.float32) + arrived[2 + at][...].astype(jnp.float32)
        out_ref[band] = (base_ref[band] + gate_ref[...] * total).astype(jnp.bfloat16)


def local(
    text_states,
    image_states,
    counts,
    norm_gain,
    w_query,
    q_gain,
    w_key,
    w_value,
    k_gain,
    w_out,
    attn_gate,
):
    tp_me = lax.axis_index("tp")
    ctx_me = lax.axis_index("ctx")
    ctx_row = ctx_me.astype(jnp.int32).reshape(1)
    me = jnp.stack([ctx_me, tp_me]).astype(jnp.int32)

    cut = cut_weights(ctx_me, tp_me, w_out)
    image_states, text_first, cut = lax.optimization_barrier((image_states, text_states, cut))
    piece = tp_send(cut, (0, 1))
    sent = project_kv(image_states.T, w_key, w_value)
    sent, piece = lax.optimization_barrier((sent, piece))
    mine = [piece] + [ctx_send(piece, (ring, 0, 0)) for ring in RING]
    arrived = lax.all_to_all(sent, "tp", 0, 0, tiled=True)
    query = project_query(text_first, norm_gain, w_query, q_gain)
    arrived, query = lax.optimization_barrier((arrived, query))
    own_kv = combine_kv(k_gain, arrived)

    far = [ctx_send(own_kv, shift + (0,)) for shift in AROUND[:-1]] + [own_kv]
    near = [ctx_send(block, (0, 0, 1)) for block in far]
    far[0], *mine = lax.optimization_barrier((far[0], *mine))
    held = attend(ctx_row, counts, query, far, 0)
    (attended,) = attend(ctx_row, counts, query, near, 1, held)
    other = [ctx_send(block, (0, 0, 1)) for block in mine]

    gate = jnp.tanh(attn_gate).reshape(1, 1)
    swapped = tp_send(attended, (0, 1))
    own = project_own(me, gate, attended, w_out, text_states)
    rows = text_states.shape[0]
    low, high = (0, rows // 2), (rows // 2, rows)
    operands = (me, gate, swapped, own, mine, other)
    (first_low,) = project_out([((1, 2), *low)], jnp.bfloat16, *operands)
    low_arrived = hop_send(first_low, 1)
    (first_high,) = project_out([((3, 2), *high)], jnp.bfloat16, *operands)
    high_arrived = hop_send(first_high, 3)
    kept_low, kept_high, base = project_out([((3,), *low), ((1,), *high), ((0,), 0, rows)], jnp.float32, *operands)
    low_last = hop_send(relay(kept_low, low_arrived), 3)
    high_last = hop_send(relay(kept_high, high_arrived), 1)
    arrived = [low_arrived, high_arrived, low_last, high_last]
    return pl.pallas_call(
        add_kernel,
        out_shape=jax.ShapeDtypeStruct(base.shape, jnp.bfloat16),
        in_specs=[VMEM] * (2 + len(arrived)),
        out_specs=VMEM,
        compiler_params=params(16),
        cost_estimate=HINT,
        name="add_residual",
    )(base, gate, *arrived)


def solution(mesh):
    in_specs = (
        P("ctx", None),
        P("ctx", "tp"),
        P(),
        P(),
        P(None, "tp"),
        P(),
        P("tp", None),
        P("tp", None),
        P(),
        P("tp", None),
        P(),
    )
    out_specs = P("ctx", "tp")
    return jax.shard_map(local, mesh=mesh, in_specs=in_specs, out_specs=out_specs, check_vma=False)
```

time: 137 us -> 117 us (0.85)
  waiting for transfers between devices: 54.1 us -> 37.3 us
  Pallas kernels: 44.3 us -> 28.3 us
  starting transfers between devices: 29.5 us -> 39.9 us
  local copies, waits for them, and re-layouts: 7.54 us -> 9.73 us
    ppermute x0 -> x4, waiting for transfers between devices: none -> 19.3 us  [hop_send(): return lax.ppermute(block, 'tp', [(i, i ^ 2 * hop) for i in range(8)])]
    ppermute x5 -> x2, waiting for transfers between devices: 22.7 us -> 6.86 us  [tp_send(): return lax.ppermute(block, 'tp', [(i, tp_dest(i, shift)) for i in range(8)])]
    pallas_call x8, Pallas kernels: 33.1 us -> 18.5 us  [the longest x2 8.34 us: attend(): pl.pallas_call(functools.partial(attend_kernel, flip, bool(held)), out_sh...]
    all_to_all x1, waiting for transfers between devices: 14.8 us -> 3.26 us  [local(): arrived = lax.all_to_all(sent, 'tp', 0, 0, tiled=True)]
    ppermute x15 -> x22, waiting for transfers between devices: 16.7 us -> 7.89 us  [ctx_send(): lax.ppermute(block, 'ctx', [(i, ctx_dest(i, shift)) for i in range(16)])]
    ppermute x15 -> x22, starting transfers between devices: 17.4 us -> 24.4 us  [ctx_send(): lax.ppermute(block, 'ctx', [(i, ctx_dest(i, shift)) for i in range(16)])]
    ppermute x0 -> x4, starting transfers between devices: none -> 4.82 us  [hop_send(): return lax.ppermute(block, 'tp', [(i, i ^ 2 * hop) for i in range(8)])]
    ppermute x5 -> x2, starting transfers between devices: 6.65 us -> 4.11 us  [tp_send(): return lax.ppermute(block, 'tp', [(i, tp_dest(i, shift)) for i in range(8)])]
  transfers between devices with their start and end apart: 21 -> 29, of which waited for: 10 -> 15; matrix products, arithmetic and copies ran while one was open for 0% -> 0% of each run, Pallas kernels for 31% -> 22%
where the time goes in v2:
time: 117 us; the launch traced here: 116 us
  starting transfers between devices  39.9 us (34%)
  waiting for transfers between devices  37.3 us (32%)
  Pallas kernels  28.3 us (24%)
  local copies, waits for them, and re-layouts  9.73 us (8%)
    ppermute x22, starting transfers between devices, ctx_send(): lax.ppermute(block, 'ctx', [(i, ctx_dest(i, shift)) for i in range(16)])  24.4 us
    ppermute x4, waiting for transfers between devices, hop_send(): return lax.ppermute(block, 'tp', [(i, i ^ 2 * hop) for i in range(8)])  19.3 us
    pallas_call x2, Pallas kernels, attend(): pl.pallas_call(functools.partial(attend_kernel, flip, bool(held)), out_sh...  8.34 us
    unnamed x16, local copies, waits for them, and re-layouts  8.24 us
    ppermute x22, waiting for transfers between devices, ctx_send(): lax.ppermute(block, 'ctx', [(i, ctx_dest(i, shift)) for i in range(16)])  7.89 us
    ppermute x2, waiting for transfers between devices, tp_send(): return lax.ppermute(block, 'tp', [(i, tp_dest(i, shift)) for i in range(8)])  6.86 us
    all_to_all x1, starting transfers between devices, local(): arrived = lax.all_to_all(sent, 'tp', 0, 0, tiled=True)  6.49 us
    pallas_call x1, Pallas kernels, project_query(): pl.pallas_call(query_kernel, out_shape=jax.ShapeDtypeStruct((rows * width...  5.17 us
  transfers between devices with their start and end apart: 29, of which 15 were waited for; matrix products, arithmetic and copies ran while one was open for 0% of the time, Pallas kernels for 22%

profile of v2, /device:TPU:0, one launch (start us, length us, event | category | flops | bytes accessed | tf_op | source)
XLA Modules:
  0.0 116.2 jit_solution(13841641476977875290)
XLA Ops:
  5.9 4.5 %project_kv.1 = bf16[8,384,256]{2,1,0:T(8,128)(2,1)} custom-call(bf16[960,384]{1,0:T(8,128)(2,1)S(1)} %bitcast.7, bf16[960,1024]{1,0:T(8,128)(2,1)S(1)} %copy-done.2, bf16[960,1024]{1,0:T(8,128)(2,1)} %value_ref.1), custom_call_target="tpu_custom_call" | custom-call | flops 1048576 | bytes 1024 | tf_op jit(solution)/shard_map/project_kv/pallas_call | solution.py:62
  10.4 4.7 %collective-permute-done.refs_4_ = bf16[128,2048]{1,0:T(8,128)(2,1)S(1)} collective-permute-done((bf16[128,2048]{1,0:T(8,128)(2,1)S(1)}, bf16[128,2048]{1,0:T(8,128)(2,1)S(1)}, u32[]{:S(2)}, u32[]{:S(2)}) %collective-permute-start) | collective-permute-done | bytes 524320 | tf_op jit(solution)/shard_map/ppermute | solution.py:33
  15.1 6.5 %all-to-all-start = ((bf16[8,384,256]{2,1,0:T(8,128)(2,1)}), bf16[8,384,256]{2,1,0:T(8,128)(2,1)S(1)}, u32[]{:S(2)}, u32[]{:S(2)}) async-start(bf16[8,384,256]{2,1,0:T(8,128)(2,1)} %project_kv.1), calls=%async_computation | async-start | bytes 3145728 | tf_op jit(solution)/shard_map/all_to_all | solution.py:341
  21.6 3.2 %collective-permute-start.16 = (bf16[128,2048]{1,0:T(8,128)(2,1)S(1)}, bf16[128,2048]{1,0:T(8,128)(2,1)S(1)}, u32[]{:S(2)}, u32[]{:S(2)}) collective-permute-start(bf16[128,2048]{1,0:T(8,128)(2,1)S(1)} %collective-permute-done.refs_4_), channel_id=1, source_target_pairs={{0,64},{8,72},{16,80},{24,88},{32,96},{40,104},{48,112},{56,120},{... | collective-permute-start | bytes 1572872 | tf_op jit(solution)/shard_map/ppermute | solution.py:41
  25.5 2.6 %collective-permute-start.18 = (bf16[128,2048]{1,0:T(8,128)(2,1)S(1)}, bf16[128,2048]{1,0:T(8,128)(2,1)}, u32[]{:S(2)}, u32[]{:S(2)}) collective-permute-start(bf16[128,2048]{1,0:T(8,128)(2,1)S(1)} %collective-permute-done.refs_4_), channel_id=1, source_target_pairs={{0,96},{8,104},{16,112},{24,120},{32,0},{40,8},{48,16},{56,24},{64... | collective-permute-start | bytes 1572872 | tf_op jit(solution)/shard_map/ppermute | solution.py:41
  28.1 2.2 %copy-done = bf16[256,8192]{1,0:T(8,128)(2,1)S(1)} copy-done((bf16[256,8192]{1,0:T(8,128)(2,1)S(1)}, bf16[256,8192]{1,0:T(8,128)(2,1)}, u32[]{:S(2)}) %copy-start) | copy-done | bytes 4194328
  30.2 3.4 %copy-done.1 = bf16[8192,512]{1,0:T(8,128)(2,1)S(1)} copy-done((bf16[8192,512]{1,0:T(8,128)(2,1)S(1)}, bf16[8192,512]{1,0:T(8,128)(2,1)}, u32[]{:S(2)}) %copy-start.1) | copy-done | bytes 8388632
  33.6 5.2 %project_query.1.query_ref = bf16[1024,128]{1,0:T(8,128)(2,1)S(1)} custom-call(bf16[256,8192]{1,0:T(8,128)(2,1)S(1)} %copy-done, f32[1,8192]{1,0:T(1,128)S(1)} %bitcast.8, bf16[8192,512]{1,0:T(8,128)(2,1)S(1)} %copy-done.1, f32[1,128]{1,0:T(1,128)S(1)} %bitcast.9), custom_call_target="tpu_custom_call" | custom-call | flops 1048576 | bytes 1024 | tf_op jit(solution)/shard_map/project_query/pallas_call | solution.py:104
  38.8 3.3 %all-to-all-done.parts_ref = bf16[8,384,256]{2,1,0:T(8,128)(2,1)S(1)} async-done(((bf16[8,384,256]{2,1,0:T(8,128)(2,1)}), bf16[8,384,256]{2,1,0:T(8,128)(2,1)S(1)}, u32[]{:S(2)}, u32[]{:S(2)}) %all-to-all-start) | async-done | bytes 1572896 | tf_op jit(solution)/shard_map/all_to_all | solution.py:341
  42.4 5.4 %collective-permute-start.1 = (bf16[384,256]{1,0:T(8,128)(2,1)S(1)}, bf16[384,256]{1,0:T(8,128)(2,1)S(1)}, u32[]{:S(2)}, u32[]{:S(2)}) collective-permute-start(bf16[384,256]{1,0:T(8,128)(2,1)S(1)} %combine_kv.1.refs_7_), channel_id=1, source_target_pairs={{0,80},{8,88},{16,64},{24,72},{32,112},{40,120},{48,96},{56,104},{... | collective-permute-start | bytes 589832 | tf_op jit(solution)/shard_map/ppermute | solution.py:41
  48.7 4.7 %collective-permute-start.13 = (bf16[384,256]{1,0:T(8,128)(2,1)S(1)}, bf16[384,256]{1,0:T(8,128)(2,1)S(1)}, u32[]{:S(2)}, u32[]{:S(2)}) collective-permute-start(bf16[384,256]{1,0:T(8,128)(2,1)S(1)} %combine_kv.1.refs_7_), channel_id=1, source_target_pairs={{0,112},{8,120},{16,96},{24,104},{32,16},{40,24},{48,0},{56,8},{64... | collective-permute-start | bytes 589832 | tf_op jit(solution)/shard_map/ppermute | solution.py:41
  54.7 3.0 %collective-permute-start.5 = (bf16[384,256]{1,0:T(8,128)(2,1)S(1)}, bf16[384,256]{1,0:T(8,128)(2,1)S(1)}, u32[]{:S(2)}, u32[]{:S(2)}) collective-permute-start(bf16[384,256]{1,0:T(8,128)(2,1)S(1)} %combine_kv.1.refs_7_), channel_id=1, source_target_pairs={{0,32},{8,40},{16,48},{24,56},{32,64},{40,72},{48,80},{56,88},{64,... | collective-permute-start | bytes 589832 | tf_op jit(solution)/shard_map/ppermute | solution.py:41
  57.7 1.7 %collective-permute-done.11.refs_5_ = bf16[384,256]{1,0:T(8,128)(2,1)S(1)} collective-permute-done((bf16[384,256]{1,0:T(8,128)(2,1)S(1)}, bf16[384,256]{1,0:T(8,128)(2,1)S(1)}, u32[]{:S(2)}, u32[]{:S(2)}) %collective-permute-start.11) | collective-permute-done | bytes 196640 | tf_op jit(solution)/shard_map/ppermute | solution.py:41
  68.3 4.1 %attend.2 = (f32[1024,256]{1,0:T(8,128)S(1)}, f32[1024,128]{1,0:T(8,128)S(1)}) custom-call(s32[1]{0:T(128)} %bitcast.me_ref, s32[16]{0:T(128)S(1)} %copy-done.5, bf16[1024,128]{1,0:T(8,128)(2,1)S(1)} %project_query.1.query_ref, bf16[384,256]{1,0:T(8,128)(2,1)S(1)} %collective-permute-done.1.refs_0_, bf16[384,256]{1,0:T(8,128)(2,1)S(1)} %collective-permute-done.3.refs_1_, ...), custom_call_target="tpu_custom_call" | custom-call | flops 1048576 | bytes 1024 | tf_op jit(solution)/shard_map/attend/pallas_call | solution.py:192
  72.3 4.3 %attend.3.attended_ref = bf16[256,512]{1,0:T(8,128)(2,1)S(1)} custom-call(s32[1]{0:T(128)} %bitcast.me_ref, s32[16]{0:T(128)S(1)} %copy-done.5, bf16[1024,128]{1,0:T(8,128)(2,1)S(1)} %project_query.1.query_ref, bf16[384,256]{1,0:T(8,128)(2,1)S(1)} %collective-permute-done.2.refs_0_, bf16[384,256]{1,0:T(8,128)(2,1)S(1)} %collective-permute-done.4.refs_1_, ...), custom_call_target="tpu_custom_call" | custom-call | flops 1048576 | bytes 1024 | tf_op jit(solution)/shard_map/attend/pallas_call | solution.py:192
  76.6 2.5 %collective-permute-start.19 = (bf16[256,512]{1,0:T(8,128)(2,1)S(1)}, bf16[256,512]{1,0:T(8,128)(2,1)S(1)}, u32[]{:S(2)}, u32[]{:S(2)}) collective-permute-start(bf16[256,512]{1,0:T(8,128)(2,1)S(1)} %attend.3.attended_ref), channel_id=1, source_target_pairs={{0,1},{1,0},{2,3},{3,2},{4,5},{5,4},{6,7},{7,6},{8,9},{9,8},{10,11... | collective-permute-start | bytes 786440 | tf_op jit(solution)/shard_map/ppermute | solution.py:33
  79.9 3.8 %project_own.1 = (f32[256,1024]{1,0:T(8,128)S(1)}, f32[256,1024]{1,0:T(8,128)S(1)}, f32[256,1024]{1,0:T(8,128)S(1)}, f32[256,1024]{1,0:T(8,128)S(1)}) custom-call(s32[2]{0:T(128)S(1)} %pad_add_fusion.me_ref, f32[1,1]{1,0:T(1,128)} %bitcast.2.gate_ref, bf16[256,512]{1,0:T(8,128)(2,1)S(1)} %attend.3.attended_ref, bf16[512,8192]{1,0:T(8,128)(2,1)} %weight_ref.3, ...), custom_call_target="tpu_custom_call" | custom-call | flops 1048576 | bytes 1024 | tf_op jit(solution)/shard_map/project_own/pallas_call | solution.py:240
  83.7 2.2 %collective-permute-done.19.swapped_ref = bf16[256,512]{1,0:T(8,128)(2,1)S(1)} collective-permute-done((bf16[256,512]{1,0:T(8,128)(2,1)S(1)}, bf16[256,512]{1,0:T(8,128)(2,1)S(1)}, u32[]{:S(2)}, u32[]{:S(2)}) %collective-permute-start.19) | collective-permute-done | bytes 262176 | tf_op jit(solution)/shard_map/ppermute | solution.py:33
  87.4 3.9 %collective-permute-start.25 = (bf16[256,1024]{1,0:T(8,128)(2,1)S(1)}, bf16[256,1024]{1,0:T(8,128)(2,1)S(1)}, u32[]{:S(2)}, u32[]{:S(2)}) collective-permute-start(bf16[256,1024]{1,0:T(8,128)(2,1)S(1)} %project_out.5), channel_id=1, source_target_pairs={{0,6},{1,7},{2,4},{3,5},{4,2},{5,3},{6,0},{7,1},{8,14},{9,15},{10,... | collective-permute-start | bytes 1572872 | tf_op jit(solution)/shard_map/ppermute | solution.py:37
  93.3 1.8 %project_out.3 = (f32[128,1024]{1,0:T(8,128)S(1)}, f32[128,1024]{1,0:T(8,128)S(1)}, f32[256,1024]{1,0:T(8,128)S(1)}) custom-call(s32[2]{0:T(128)S(1)} %pad_add_fusion.me_ref, f32[1,1]{1,0:T(1,128)} %bitcast.2.gate_ref, bf16[256,512]{1,0:T(8,128)(2,1)S(1)} %collective-permute-done.19.swapped_ref, f32[256,1024]{1,0:T(8,128)S(1)} %get-tuple-element.36.refs_0_, ...), custom_call_target="tpu_custom_call" | custom-call | flops 1048576 | bytes 1024 | tf_op jit(solution)/shard_map/project_out/pallas_call | solution.py:280
  95.1 7.7 %collective-permute-done.25.arrived_ref.refs_1_ = bf16[256,1024]{1,0:T(8,128)(2,1)S(1)} collective-permute-done((bf16[256,1024]{1,0:T(8,128)(2,1)S(1)}, bf16[256,1024]{1,0:T(8,128)(2,1)S(1)}, u32[]{:S(2)}, u32[]{:S(2)}) %collective-permute-start.25) | collective-permute-done | bytes 524320 | tf_op jit(solution)/shard_map/ppermute | solution.py:37
  103.3 4.0 %collective-permute-done.24.arrived_ref.refs_0_ = bf16[256,1024]{1,0:T(8,128)(2,1)S(1)} collective-permute-done((bf16[256,1024]{1,0:T(8,128)(2,1)S(1)}, bf16[256,1024]{1,0:T(8,128)(2,1)S(1)}, u32[]{:S(2)}, u32[]{:S(2)}) %collective-permute-start.24) | collective-permute-done | bytes 524320 | tf_op jit(solution)/shard_map/ppermute | solution.py:37
  107.5 4.0 %collective-permute-done.27.refs_3_ = bf16[128,1024]{1,0:T(8,128)(2,1)S(1)} collective-permute-done((bf16[128,1024]{1,0:T(8,128)(2,1)S(1)}, bf16[128,1024]{1,0:T(8,128)(2,1)S(1)}, u32[]{:S(2)}, u32[]{:S(2)}) %collective-permute-start.27) | collective-permute-done | bytes 262176 | tf_op jit(solution)/shard_map/ppermute | solution.py:37
  111.5 3.5 %collective-permute-done.26.refs_2_ = bf16[128,1024]{1,0:T(8,128)(2,1)S(1)} collective-permute-done((bf16[128,1024]{1,0:T(8,128)(2,1)S(1)}, bf16[128,1024]{1,0:T(8,128)(2,1)S(1)}, u32[]{:S(2)}, u32[]{:S(2)}) %collective-permute-start.26) | collective-permute-done | bytes 262176 | tf_op jit(solution)/shard_map/ppermute | solution.py:37
  (65 shorter events, 23.1 us)
Async XLA Ops:
  1.5 13.6 %collective-permute-start = (bf16[128,2048]{1,0:T(8,128)(2,1)S(1)}, bf16[128,2048]{1,0:T(8,128)(2,1)S(1)}, u32[]{:S(2)}, u32[]{:S(2)}) collective-permute-start(bf16[128,2048]{1,0:T(8,128)(2,1)S(1)} %pad_maximum_fusion), channel_id=1, source_target_pairs={{0,1},{1,0},{2,3},{3,2},{4,5},{5,4},{6,7},{7,6},{8,9},{9,8},{10,11... | collective-permute-start | bytes 1572872 | tf_op jit(solution)/shard_map/ppermute | solution.py:33
  15.1 26.9 %all-to-all-start = ((bf16[8,384,256]{2,1,0:T(8,128)(2,1)}), bf16[8,384,256]{2,1,0:T(8,128)(2,1)S(1)}, u32[]{:S(2)}, u32[]{:S(2)}) async-start(bf16[8,384,256]{2,1,0:T(8,128)(2,1)} %project_kv.1), calls=%async_computation | async-start | bytes 3145728 | tf_op jit(solution)/shard_map/all_to_all | solution.py:341
  21.6 27.1 %collective-permute-start.16 = (bf16[128,2048]{1,0:T(8,128)(2,1)S(1)}, bf16[128,2048]{1,0:T(8,128)(2,1)S(1)}, u32[]{:S(2)}, u32[]{:S(2)}) collective-permute-start(bf16[128,2048]{1,0:T(8,128)(2,1)S(1)} %collective-permute-done.refs_4_), channel_id=1, source_target_pairs={{0,64},{8,72},{16,80},{24,88},{32,96},{40,104},{48,112},{56,120},{... | collective-permute-start | bytes 1572872 | tf_op jit(solution)/shard_map/ppermute | solution.py:41
  24.8 28.6 %collective-permute-start.17 = (bf16[128,2048]{1,0:T(8,128)(2,1)S(1)}, bf16[128,2048]{1,0:T(8,128)(2,1)S(1)}, u32[]{:S(2)}, u32[]{:S(2)}) collective-permute-start(bf16[128,2048]{1,0:T(8,128)(2,1)S(1)} %collective-permute-done.refs_4_), channel_id=1, source_target_pairs={{0,32},{8,40},{16,48},{24,56},{32,64},{40,72},{48,80},{56,88},{64,... | collective-permute-start | bytes 1572872 | tf_op jit(solution)/shard_map/ppermute | solution.py:41
  25.5 28.0 %collective-permute-start.18 = (bf16[128,2048]{1,0:T(8,128)(2,1)S(1)}, bf16[128,2048]{1,0:T(8,128)(2,1)}, u32[]{:S(2)}, u32[]{:S(2)}) collective-permute-start(bf16[128,2048]{1,0:T(8,128)(2,1)S(1)} %collective-permute-done.refs_4_), channel_id=1, source_target_pairs={{0,96},{8,104},{16,112},{24,120},{32,0},{40,8},{48,16},{56,24},{64... | collective-permute-start | bytes 1572872 | tf_op jit(solution)/shard_map/ppermute | solution.py:41
  42.4 12.3 %collective-permute-start.1 = (bf16[384,256]{1,0:T(8,128)(2,1)S(1)}, bf16[384,256]{1,0:T(8,128)(2,1)S(1)}, u32[]{:S(2)}, u32[]{:S(2)}) collective-permute-start(bf16[384,256]{1,0:T(8,128)(2,1)S(1)} %combine_kv.1.refs_7_), channel_id=1, source_target_pairs={{0,80},{8,88},{16,64},{24,72},{32,112},{40,120},{48,96},{56,104},{... | collective-permute-start | bytes 589832 | tf_op jit(solution)/shard_map/ppermute | solution.py:41
  47.8 11.6 %collective-permute-start.11 = (bf16[384,256]{1,0:T(8,128)(2,1)S(1)}, bf16[384,256]{1,0:T(8,128)(2,1)S(1)}, u32[]{:S(2)}, u32[]{:S(2)}) collective-permute-start(bf16[384,256]{1,0:T(8,128)(2,1)S(1)} %combine_kv.1.refs_7_), channel_id=1, source_target_pairs={{0,48},{8,56},{16,32},{24,40},{32,80},{40,88},{48,64},{56,72},{64,... | collective-permute-start | bytes 589832 | tf_op jit(solution)/shard_map/ppermute | solution.py:41
  48.7 12.9 %collective-permute-start.13 = (bf16[384,256]{1,0:T(8,128)(2,1)S(1)}, bf16[384,256]{1,0:T(8,128)(2,1)S(1)}, u32[]{:S(2)}, u32[]{:S(2)}) collective-permute-start(bf16[384,256]{1,0:T(8,128)(2,1)S(1)} %combine_kv.1.refs_7_), channel_id=1, source_target_pairs={{0,112},{8,120},{16,96},{24,104},{32,16},{40,24},{48,0},{56,8},{64... | collective-permute-start | bytes 589832 | tf_op jit(solution)/shard_map/ppermute | solution.py:41
  53.4 9.2 %collective-permute-start.9 = (bf16[384,256]{1,0:T(8,128)(2,1)S(1)}, bf16[384,256]{1,0:T(8,128)(2,1)S(1)}, u32[]{:S(2)}, u32[]{:S(2)}) collective-permute-start(bf16[384,256]{1,0:T(8,128)(2,1)S(1)} %combine_kv.1.refs_7_), channel_id=1, source_target_pairs={{0,64},{8,72},{16,80},{24,88},{32,96},{40,104},{48,112},{56,120},{... | collective-permute-start | bytes 589832 | tf_op jit(solution)/shard_map/ppermute | solution.py:41
  53.5 10.5 %collective-permute-start.3 = (bf16[384,256]{1,0:T(8,128)(2,1)S(1)}, bf16[384,256]{1,0:T(8,128)(2,1)S(1)}, u32[]{:S(2)}, u32[]{:S(2)}) collective-permute-start(bf16[384,256]{1,0:T(8,128)(2,1)S(1)} %combine_kv.1.refs_7_), channel_id=1, source_target_pairs={{0,16},{8,24},{16,0},{24,8},{32,48},{40,56},{48,32},{56,40},{64,80... | collective-permute-start | bytes 589832 | tf_op jit(solution)/shard_map/ppermute | solution.py:41
  54.7 10.6 %collective-permute-start.5 = (bf16[384,256]{1,0:T(8,128)(2,1)S(1)}, bf16[384,256]{1,0:T(8,128)(2,1)S(1)}, u32[]{:S(2)}, u32[]{:S(2)}) collective-permute-start(bf16[384,256]{1,0:T(8,128)(2,1)S(1)} %combine_kv.1.refs_7_), channel_id=1, source_target_pairs={{0,32},{8,40},{16,48},{24,56},{32,64},{40,72},{48,80},{56,88},{64,... | collective-permute-start | bytes 589832 | tf_op jit(solution)/shard_map/ppermute | solution.py:41
  59.4 6.6 %collective-permute-start.7 = (bf16[384,256]{1,0:T(8,128)(2,1)S(1)}, bf16[384,256]{1,0:T(8,128)(2,1)S(1)}, u32[]{:S(2)}, u32[]{:S(2)}) collective-permute-start(bf16[384,256]{1,0:T(8,128)(2,1)S(1)} %combine_kv.1.refs_7_), channel_id=1, source_target_pairs={{0,96},{8,104},{16,112},{24,120},{32,0},{40,8},{48,16},{56,24},{64... | collective-permute-start | bytes 589832 | tf_op jit(solution)/shard_map/ppermute | solution.py:41
  61.6 4.4 %collective-permute-start.15 = (bf16[384,256]{1,0:T(8,128)(2,1)S(1)}, bf16[384,256]{1,0:T(8,128)(2,1)S(1)}, u32[]{:S(2)}, u32[]{:S(2)}) collective-permute-start(bf16[384,256]{1,0:T(8,128)(2,1)S(1)} %combine_kv.1.refs_7_), channel_id=1, source_target_pairs={{0,8},{8,0},{16,24},{24,16},{32,40},{40,32},{48,56},{56,48},{64,72... | collective-permute-start | bytes 589832 | tf_op jit(solution)/shard_map/ppermute | solution.py:41
  62.6 3.9 %collective-permute-start.10 = (bf16[384,256]{1,0:T(8,128)(2,1)S(1)}, bf16[384,256]{1,0:T(8,128)(2,1)S(1)}, u32[]{:S(2)}, u32[]{:S(2)}) collective-permute-start(bf16[384,256]{1,0:T(8,128)(2,1)S(1)} %collective-permute-done.9.refs_4_), channel_id=1, source_target_pairs={{0,8},{8,0},{16,24},{24,16},{32,40},{40,32},{48,56},{56,48},{64,72... | collective-permute-start | bytes 589832 | tf_op jit(solution)/shard_map/ppermute | solution.py:41
  66.6 19.2 %collective-permute-start.20 = (bf16[128,2048]{1,0:T(8,128)(2,1)S(1)}, bf16[128,2048]{1,0:T(8,128)(2,1)S(1)}, u32[]{:S(2)}, u32[]{:S(2)}) collective-permute-start(bf16[128,2048]{1,0:T(8,128)(2,1)S(1)} %collective-permute-done.refs_4_), channel_id=1, source_target_pairs={{0,8},{8,0},{16,24},{24,16},{32,40},{40,32},{48,56},{56,48},{64,72... | collective-permute-start | bytes 1572872 | tf_op jit(solution)/shard_map/ppermute | solution.py:41
  67.1 18.8 %collective-permute-start.21 = (bf16[128,2048]{1,0:T(8,128)(2,1)S(1)}, bf16[128,2048]{1,0:T(8,128)(2,1)S(1)}, u32[]{:S(2)}, u32[]{:S(2)}) collective-permute-start(bf16[128,2048]{1,0:T(8,128)(2,1)S(1)} %collective-permute-done.16.refs_5_), channel_id=1, source_target_pairs={{0,8},{8,0},{16,24},{24,16},{32,40},{40,32},{48,56},{56,48},{64,72... | collective-permute-start | bytes 1572872 | tf_op jit(solution)/shard_map/ppermute | solution.py:41
  67.5 18.4 %collective-permute-start.22 = (bf16[128,2048]{1,0:T(8,128)(2,1)S(1)}, bf16[128,2048]{1,0:T(8,128)(2,1)S(1)}, u32[]{:S(2)}, u32[]{:S(2)}) collective-permute-start(bf16[128,2048]{1,0:T(8,128)(2,1)S(1)} %collective-permute-done.17.refs_6_), channel_id=1, source_target_pairs={{0,8},{8,0},{16,24},{24,16},{32,40},{40,32},{48,56},{56,48},{64,72... | collective-permute-start | bytes 1572872 | tf_op jit(solution)/shard_map/ppermute | solution.py:41
  67.7 18.1 %collective-permute-start.23 = (bf16[128,2048]{1,0:T(8,128)(2,1)}, bf16[128,2048]{1,0:T(8,128)(2,1)S(1)}, u32[]{:S(2)}, u32[]{:S(2)}) collective-permute-start(bf16[128,2048]{1,0:T(8,128)(2,1)} %collective-permute-done.18.refs_7_), channel_id=1, source_target_pairs={{0,8},{8,0},{16,24},{24,16},{32,40},{40,32},{48,56},{56,48},{64,72... | collective-permute-start | bytes 1572872 | tf_op jit(solution)/shard_map/ppermute | solution.py:41
  68.0 4.3 %collective-permute-start.8 = (bf16[384,256]{1,0:T(8,128)(2,1)S(1)}, bf16[384,256]{1,0:T(8,128)(2,1)S(1)}, u32[]{:S(2)}, u32[]{:S(2)}) collective-permute-start(bf16[384,256]{1,0:T(8,128)(2,1)S(1)} %collective-permute-done.7.refs_3_), channel_id=1, source_target_pairs={{0,8},{8,0},{16,24},{24,16},{32,40},{40,32},{48,56},{56,48},{64,72... | collective-permute-start | bytes 589832 | tf_op jit(solution)/shard_map/ppermute | solution.py:41
  76.6 9.2 %collective-permute-start.19 = (bf16[256,512]{1,0:T(8,128)(2,1)S(1)}, bf16[256,512]{1,0:T(8,128)(2,1)S(1)}, u32[]{:S(2)}, u32[]{:S(2)}) collective-permute-start(bf16[256,512]{1,0:T(8,128)(2,1)S(1)} %attend.3.attended_ref), channel_id=1, source_target_pairs={{0,1},{1,0},{2,3},{3,2},{4,5},{5,4},{6,7},{7,6},{8,9},{9,8},{10,11... | collective-permute-start | bytes 786440 | tf_op jit(solution)/shard_map/ppermute | solution.py:33
  87.4 15.4 %collective-permute-start.25 = (bf16[256,1024]{1,0:T(8,128)(2,1)S(1)}, bf16[256,1024]{1,0:T(8,128)(2,1)S(1)}, u32[]{:S(2)}, u32[]{:S(2)}) collective-permute-start(bf16[256,1024]{1,0:T(8,128)(2,1)S(1)} %project_out.5), channel_id=1, source_target_pairs={{0,6},{1,7},{2,4},{3,5},{4,2},{5,3},{6,0},{7,1},{8,14},{9,15},{10,... | collective-permute-start | bytes 1572872 | tf_op jit(solution)/shard_map/ppermute | solution.py:37
  92.8 14.5 %collective-permute-start.24 = (bf16[256,1024]{1,0:T(8,128)(2,1)S(1)}, bf16[256,1024]{1,0:T(8,128)(2,1)S(1)}, u32[]{:S(2)}, u32[]{:S(2)}) collective-permute-start(bf16[256,1024]{1,0:T(8,128)(2,1)S(1)} %project_out.4), channel_id=1, source_target_pairs={{0,2},{1,3},{2,0},{3,1},{4,6},{5,7},{6,4},{7,5},{8,10},{9,11},{10,... | collective-permute-start | bytes 1572872 | tf_op jit(solution)/shard_map/ppermute | solution.py:37
  102.9 8.6 %collective-permute-start.27 = (bf16[128,1024]{1,0:T(8,128)(2,1)S(1)}, bf16[128,1024]{1,0:T(8,128)(2,1)S(1)}, u32[]{:S(2)}, u32[]{:S(2)}) collective-permute-start(bf16[128,1024]{1,0:T(8,128)(2,1)S(1)} %relay.3), channel_id=1, source_target_pairs={{0,2},{1,3},{2,0},{3,1},{4,6},{5,7},{6,4},{7,5},{8,10},{9,11},{10,... | collective-permute-start | bytes 786440 | tf_op jit(solution)/shard_map/ppermute | solution.py:37
  107.4 7.7 %collective-permute-start.26 = (bf16[128,1024]{1,0:T(8,128)(2,1)S(1)}, bf16[128,1024]{1,0:T(8,128)(2,1)S(1)}, u32[]{:S(2)}, u32[]{:S(2)}) collective-permute-start(bf16[128,1024]{1,0:T(8,128)(2,1)S(1)} %relay.2), channel_id=1, source_target_pairs={{0,6},{1,7},{2,4},{3,5},{4,2},{5,3},{6,0},{7,1},{8,14},{9,15},{10,... | collective-permute-start | bytes 786440 | tf_op jit(solution)/shard_map/ppermute | solution.py:37
  (13 other events, 104.8 us)
